TPU v7x, 256 devices: a whole 4x4x8 slice. The times are simulated.
256 devices in a mesh: gx: 32 (over z, y), dp: 8 (over x, core).
Axes of the slice: x: 4, y: 4, z: 8, core: 2. Of those that a mesh axis runs over, the one named last changes fastest.
Arguments:
- inputs: bfloat16 [8, 128, 64, 32, 128], P('dp', 'gx'), may hold values from -6 to 6
- spectral_weights: bfloat16 [32, 2, 32, 32, 256], P('gx'), may hold values from -0.75 to 0.75
- skip_weights: bfloat16 [32, 32], replicated, may hold values from -1 to 1
- cotangent: bfloat16 [8, 128, 64, 32, 128], P('dp', 'gx'), may hold values from -6 to 6
Outputs:
- outputs: bfloat16 [8, 128, 64, 32, 128], P('dp', 'gx')
- grad_inputs: bfloat16 [8, 128, 64, 32, 128], P('dp', 'gx')
- weight_grad: float32 [32, 2, 32, 32, 256], P('gx', None, 'dp')
All inputs are finite; a program needn't handle non-finite values.
Results may differ from a plain program's by a relative error of at most 0.04.
Values may be sent and summed in bfloat16 or wider, within the bound.
A program may use at most 128 MiB of HBM per device.

v0:
```python
import math

import jax
import jax.numpy as jnp
from jax import lax
from jax.sharding import PartitionSpec as P

MY = 16
MZ = 16


def signed_of(indices, count):
    return jnp.where(indices < count // 2, indices, indices - count)


def twiddle(positions, freqs, length):
    phase = positions[:, None] * freqs[None, :] % length
    angle = 2.0 * math.pi / length * phase.astype(jnp.float32)
    return (jnp.cos(angle), jnp.sin(angle))


def rotation(tables, sign_factor):
    cos_table, sin_table = tables
    upper = jnp.stack([cos_table, sign_factor * sin_table])
    lower = jnp.stack([-sign_factor * sin_table, cos_table])
    return jnp.stack([upper, lower]).astype(jnp.bfloat16)


def bdot(form, left, right):
    return jnp.einsum(form, left, right, preferred_element_type=jnp.float32)


def forward_planes(field, y_table, z_rotation):
    batch_size, slab_rows, grid_y, channels, grid_z = field.shape
    modes_y = y_table.shape[1] // 2
    modes_z = z_rotation.shape[3]
    along_y = bdot("nxycz,yk->nxckz", field, y_table).astype(jnp.bfloat16)
    along_y = along_y.reshape(batch_size, slab_rows, channels, 2, modes_y, grid_z)
    planes = bdot("nxcayz,abzk->xnbcyk", along_y, z_rotation).astype(jnp.bfloat16)
    return planes.reshape(slab_rows, batch_size, 2, channels, modes_y * modes_z)


def inverse_planes(spectral, z_rotation, y_inverse):
    slab_rows, batch_size, parts, channels, modes = spectral.shape
    modes_y = y_inverse.shape[1]
    shaped = spectral.reshape(slab_rows, batch_size, 2, channels, modes_y, modes // modes_y)
    along_z = bdot("xnacyk,abzk->nxcbyz", shaped, z_rotation).astype(jnp.bfloat16)
    return bdot("nxcbyz,byw->nxwcz", along_z, y_inverse)


def complex_mix(modes_arr, weights):

    def product(left, right):
        return bdot("knim,kiom->knom", left, right)

    real_part = product(modes_arr[:, :, 0], weights[:, 0]) - product(
        modes_arr[:, :, 1], weights[:, 1]
    )
    imag_part = product(modes_arr[:, :, 0], weights[:, 1]) + product(
        modes_arr[:, :, 1], weights[:, 0]
    )
    return jnp.stack([real_part, imag_part], axis=2)


def conj_mix(back, weights):

    def product(left, right):
        return bdot("knom,kiom->knim", left, right)

    real_part = product(back[:, :, 0], weights[:, 0]) + product(back[:, :, 1], weights[:, 1])
    imag_part = product(back[:, :, 1], weights[:, 0]) - product(back[:, :, 0], weights[:, 1])
    return jnp.stack([real_part, imag_part], axis=2)


def weight_terms(modes_arr, back):

    def outer(left, right):
        return bdot("knim,knom->kiom", left, right)

    real_part = outer(modes_arr[:, :, 0], back[:, :, 0]) + outer(modes_arr[:, :, 1], back[:, :, 1])
    imag_part = outer(modes_arr[:, :, 0], back[:, :, 1]) - outer(modes_arr[:, :, 1], back[:, :, 0])
    return jnp.stack([real_part, imag_part], axis=1)


def to_modes(planes, mode_count):
    slab_rows = planes.shape[0]
    devices = lax.axis_size("gx")
    length = slab_rows * devices
    owned = mode_count // devices
    first_row = lax.axis_index("gx") * slab_rows

    def term(start, count):
        freqs = signed_of(jnp.arange(count, dtype=jnp.int32), mode_count)
        positions = first_row + jnp.arange(slab_rows, dtype=jnp.int32)
        table = rotation(twiddle(positions, freqs, length), -1.0)
        return bdot("xnacm,abxk->knbcm", planes, table)

    return lax.psum_scatter(
        term(jnp.int32(0), owned * lax.axis_size("gx")).astype(jnp.bfloat16),
        "gx",
        scatter_dimension=0,
        tiled=True,
    ).astype(jnp.float32)


def to_slabs(spectral, slab_rows, mode_count):
    devices = lax.axis_size("gx")
    length = slab_rows * devices
    owned = spectral.shape[0]
    first_mode = lax.axis_index("gx") * owned
    freqs = signed_of(first_mode + jnp.arange(owned, dtype=jnp.int32), mode_count)

    def term(start, count):
        positions = jnp.arange(count, dtype=jnp.int32)
        table = rotation(twiddle(positions, freqs, length), 1.0)
        return bdot("knacm,abxk->xnbcm", spectral, table)

    return lax.psum_scatter(
        term(jnp.int32(0), slab_rows * lax.axis_size("gx")).astype(jnp.bfloat16),
        "gx",
        scatter_dimension=0,
        tiled=True,
    ).astype(jnp.float32)


def per_device(inputs, spectral_weights, skip_weights, cotangent):
    batch_size, slab_rows, grid_y, channels, grid_z = inputs.shape
    mode_count = spectral_weights.shape[0] * lax.axis_size("gx")
    modes_y = MY
    modes_z = MZ
    grid_x = slab_rows * lax.axis_size("gx")
    y_pair = twiddle(
        jnp.arange(grid_y, dtype=jnp.int32),
        signed_of(jnp.arange(modes_y, dtype=jnp.int32), modes_y),
        grid_y,
    )
    y_table = jnp.concatenate([y_pair[0], -y_pair[1]], axis=1).astype(jnp.bfloat16)
    y_inverse = jnp.stack([y_pair[0].T, -y_pair[1].T]).astype(jnp.bfloat16)
    z_pair = twiddle(
        jnp.arange(grid_z, dtype=jnp.int32), jnp.arange(modes_z, dtype=jnp.int32), grid_z
    )
    z_forward = rotation(z_pair, -1.0)
    z_backward = rotation(z_pair, 1.0)
    grid_scale = 1.0 / math.sqrt(grid_x * grid_y * grid_z)
    mode_scale = 1.0 / math.sqrt(mode_count * modes_y * modes_z)
    planes = forward_planes(inputs, y_table, z_forward)
    modes_arr = (to_modes(planes, mode_count) * grid_scale).astype(jnp.bfloat16)
    mixed = complex_mix(modes_arr, spectral_weights).astype(jnp.bfloat16)
    slab = to_slabs(mixed, slab_rows, mode_count).astype(jnp.bfloat16)
    skip_term = bdot("nxycz,cd->nxydz", inputs, skip_weights)
    pre = inverse_planes(slab, z_backward, y_inverse) * mode_scale + skip_term
    activated, pullback = jax.vjp(jax.nn.gelu, pre)
    gpre = pullback(cotangent.astype(jnp.float32))[0].astype(jnp.bfloat16)
    gplanes = forward_planes(gpre, y_table, z_forward)
    back = (to_modes(gplanes, mode_count) * mode_scale).astype(jnp.bfloat16)
    back_modes = conj_mix(back, spectral_weights).astype(jnp.bfloat16)
    terms = weight_terms(modes_arr, back)
    weight_grad = lax.psum_scatter(
        terms.astype(jnp.bfloat16), "dp", scatter_dimension=2, tiled=True
    ).astype(jnp.float32)
    gslab = to_slabs(back_modes, slab_rows, mode_count).astype(jnp.bfloat16)
    grad_field = inverse_planes(gslab, z_backward, y_inverse) * grid_scale + bdot(
        "nxydz,cd->nxycz", gpre, skip_weights
    )
    return (activated.astype(jnp.bfloat16), grad_field.astype(jnp.bfloat16), weight_grad)


def solution(mesh):
    in_specs = (
        P("dp", "gx", None, None, None),
        P("gx", None, None, None, None),
        P(),
        P("dp", "gx", None, None, None),
    )
    out_specs = (
        P("dp", "gx", None, None, None),
        P("dp", "gx", None, None, None),
        P("gx", None, "dp", None, None),
    )
    return jax.shard_map(
        per_device, mesh=mesh, in_specs=in_specs, out_specs=out_specs, check_vma=False
    )
```

profile of v0, /device:TPU:1, one launch (start us, length us, event | category | flops | bytes accessed | tf_op | source)
XLA Modules:
  0.0 996.6 jit_solution(4931222770141963676)
XLA Ops:
  9.6 1.8 fusion.23
  13.3 1.6 copy.90
  15.1 212.3 %reduce-scatter.8.cloned.1.call-done = bf16[1,1,2,32,256]{4,3,2,1,0:T(8,128)(2,1)} async-done(((bf16[32,1,2,32,256]{4,3,2,1,0:T(8,128)(2,1)}), bf16[1,1,2,32,256]{4,3,2,1,0:T(8,128)(2,1)}) %reduce-scatter.8.cloned.1.call-update) | async-done | bytes 32784 | tf_op jit(solution)/shard_map/reduce_scatter | solution.py:98
  228.6 1.3 convert_bitcast_fusion.1
  229.9 4.4 copy.93
  235.0 2.7 fusion.71
  237.7 216.8 %reduce-scatter.10.cloned.1.call-done = bf16[4,1,2,32,256]{4,3,2,1,0:T(8,128)(2,1)} async-done(((bf16[128,1,2,32,256]{4,3,2,1,0:T(8,128)(2,1)}), bf16[4,1,2,32,256]{4,3,2,1,0:T(8,128)(2,1)}) %reduce-scatter.10.cloned.1.call-update) | async-done | bytes 131088 | tf_op jit(solution)/shard_map/reduce_scatter | solution.py:118
  454.4 1.9 copy.94
  456.3 1.5 fusion.19
  457.9 8.8 fusion.15
  466.7 1.3 copy-done.1
  468.4 1.8 fusion.24
  472.0 1.6 copy.103
  473.6 211.9 %reduce-scatter.12.cloned.1.call-done = bf16[1,1,2,32,256]{4,3,2,1,0:T(8,128)(2,1)} async-done(((bf16[32,1,2,32,256]{4,3,2,1,0:T(8,128)(2,1)}), bf16[1,1,2,32,256]{4,3,2,1,0:T(8,128)(2,1)}) %reduce-scatter.12.cloned.1.call-update) | async-done | bytes 32784 | tf_op jit(solution)/shard_map/reduce_scatter | solution.py:98
  690.2 4.3 copy.106
  696.4 4.4 copy.113
  700.9 3.3 fusion.11
  704.2 52.8 %all-reduce.3.cloned.1.call-done = bf16[1,2,32,32,256]{4,3,2,1,0:T(8,128)(2,1)} async-done(((bf16[1,2,32,32,256]{4,3,2,1,0:T(8,128)(2,1)}), bf16[1,2,32,32,256]{4,3,2,1,0:T(8,128)(2,1)}) %all-reduce.3.cloned.1.call-update) | async-done | bytes 1048592
  757.0 1.6 dynamic-slice_convert_fusion
  758.6 220.0 %reduce-scatter.14.cloned.1.call-done = bf16[4,1,2,32,256]{4,3,2,1,0:T(8,128)(2,1)} async-done(((bf16[128,1,2,32,256]{4,3,2,1,0:T(8,128)(2,1)}), bf16[4,1,2,32,256]{4,3,2,1,0:T(8,128)(2,1)}) %reduce-scatter.14.cloned.1.call-update) | async-done | bytes 131088 | tf_op jit(solution)/shard_map/reduce_scatter | solution.py:118
  978.6 1.9 copy.107
  980.5 1.5 fusion.20
  982.1 5.3 fusion.10
  987.4 2.7 copy.114
  (60 shorter events, 14.4 us)
Async XLA Ops:
  7.2 1.6 copy-start
  7.2 220.2 %reduce-scatter.8.cloned.1.call-start = ((), (), s32[]{:S(2)}) async-start(), calls=%async_computation.4 | async-start | bytes 1081344 | tf_op jit(solution)/shard_map/reduce_scatter | solution.py:98
  9.5 218.6 %copy-start.3 = (bf16[1,2,32,32,256]{4,3,2,1,0:T(8,128)(2,1)S(1)}, bf16[1,2,32,32,256]{4,3,2,1,0:T(8,128)(2,1)}, u32[]{:S(2)}) copy-start(bf16[1,2,32,32,256]{4,3,2,1,0:T(8,128)(2,1)} %param.5) | copy-start | bytes 3145732
  14.8 439.6 %reduce-scatter.10.cloned.1.call-start = ((), (), s32[]{:S(2)}) async-start(), calls=%async_computation.5 | async-start | bytes 4325376 | tf_op jit(solution)/shard_map/reduce_scatter | solution.py:118
  234.3 0.7 copy-start.4
  234.3 451.2 %reduce-scatter.12.cloned.1.call-start = ((), (), s32[]{:S(2)}) async-start(), calls=%async_computation.6 | async-start | bytes 1081344 | tf_op jit(solution)/shard_map/reduce_scatter | solution.py:98
  466.7 1.3 copy-start.1
  473.5 283.5 %all-reduce.3.cloned.1.call-start = ((), (), s32[]{:S(2)}) async-start(), calls=%async_computation.8 | async-start | bytes 2097152
  687.7 290.9 %reduce-scatter.14.cloned.1.call-start = ((), (), s32[]{:S(2)}) async-start(), calls=%async_computation.7 | async-start | bytes 4325376 | tf_op jit(solution)/shard_map/reduce_scatter | solution.py:118
  694.5 0.7 copy-start.5
  696.4 4.4 copy-start.2
Sparse Core Ops, SparseCore 0:
  15.0 212.3 reduce-scatter.7
  234.4 219.9 reduce-scatter.9
  473.7 211.7 reduce-scatter.11
  687.8 69.1 all-reduce.2
  761.2 217.3 reduce-scatter.13
where the time goes:
time: 1000 us; the launch traced here: 997 us
  waiting for transfers between devices  914 us (91%)
  matrix products  31.5 us (3%)
  local copies, waits for them, and re-layouts  29.5 us (3%)
  between operations  14.7 us (1%)
    reduce_scatter x2, waiting for transfers between devices, to_slabs(): lax.psum_scatter(term(jnp.int32(0), slab_rows * lax.axis_size('gx')).asty...  437 us
    reduce_scatter x2, waiting for transfers between devices, to_modes(): lax.psum_scatter(term(jnp.int32(0), owned * lax.axis_size('gx')).astype(j...  424 us
    unnamed x6, waiting for transfers between devices  52.9 us
    dot_general x14, matrix products, bdot(): return jnp.einsum(form, left, right, preferred_element_type=jnp.float32)  31.5 us
  transfers between devices with their start and end apart: 5, of which 5 were waited for; matrix products, arithmetic and copies ran while one was open for 2% of the time, Pallas kernels for 0%

commit v1 on v0

v1 whole, which is shorter than its diff:
```python
import functools
import math

import jax
import jax.numpy as jnp
import ml_dtypes
import numpy as np
from jax import lax
from jax.experimental import pallas as pl
from jax.experimental.pallas import tpu as pltpu
from jax.sharding import PartitionSpec as P

MESH = pl.DeviceIdType.MESH
F32 = jnp.float32
BF16 = jnp.bfloat16

NX, NY, NZ, MX, MY, MZ, C = 128, 64, 128, 32, 16, 16, 32
GX, DP = 32, 8
SLAB = NX // GX
GRID_SCALE = 1.0 / math.sqrt(NX * NY * NZ)
MODE_SCALE = 1.0 / math.sqrt(MX * MY * MZ)
PIECE = (GX, 16, 128)


def angles(length, freqs):
    phase = (np.arange(length)[:, None] * freqs[None, :]) % length
    angle = np.float32(2.0 * math.pi / length) * phase.astype(np.float32)
    return np.cos(angle).astype(np.float32), np.sin(angle).astype(np.float32)


def signed(count):
    k = np.arange(count)
    return np.where(k < count // 2, k, k - count)


def tables():
    bf = ml_dtypes.bfloat16
    cz, sz = angles(NZ, np.arange(MZ))
    zt = np.zeros((MZ, 2, 8, 8, NZ), np.float32)
    for q in range(8):
        zt[:, 0, q, q, :] = cz.T
        zt[:, 1, q, q, :] = -sz.T
    cy, sy = angles(NY, signed(MY))
    yb = np.stack([cy, -sy], axis=1)
    lt = np.einsum("ybk,cd->ycbkd", yb, np.eye(16, dtype=np.float32))
    cx, sx = angles(NX, signed(MX))
    rot = np.stack([np.stack([cx, sx]), np.stack([-sx, cx])])
    rot = rot.reshape(2, 2, GX, SLAB, MX)
    xf = np.einsum("pagrk,hj->phkgajr", rot, np.eye(2, dtype=np.float32))
    xf = xf.reshape(128, 512)
    return (
        zt.reshape(256, 1024).astype(bf),
        lt.reshape(1024, 512).astype(bf),
        xf.astype(bf),
        np.ascontiguousarray(xf.T).astype(bf),
    )


def dot(a, b):
    return jnp.dot(a, b, preferred_element_type=F32)


def dot_nt(a, b):
    return lax.dot_general(a, b, (((1,), (1,)), ((), ())), preferred_element_type=F32)


def iota(shape, axis):
    return lax.broadcasted_iota(jnp.int32, shape, axis)


def swap16(x):
    _, rows, _ = x.shape
    for s in (1, 2, 4, 8):
        keep_low = (iota((rows, 128), 1) & s) == 0
        parts = [None] * 16
        for i in range(16):
            if i & s:
                continue
            low, high = x[i], x[i + s]
            parts[i] = jnp.where(keep_low, low, pltpu.roll(high, s, 1))
            parts[i + s] = jnp.where(keep_low, pltpu.roll(low, 128 - s, 1), high)
        x = parts if s == 8 else _Stack(parts, rows)
    return x


class _Stack:
    def __init__(self, parts, rows):
        self.parts, self.shape = parts, (16, rows, 128)

    def __getitem__(self, i):
        return self.parts[i]


def gelu_pair(x):
    k0 = math.sqrt(2.0 / math.pi)
    x2 = x * x
    t = jnp.tanh(k0 * (x + 0.044715 * (x2 * x)))
    half = 0.5 * (1.0 + t)
    slope = half + (0.5 * k0) * x * (1.0 - t * t) * (1.0 + (3.0 * 0.044715) * x2)
    return x * half, slope


def kernel(
    x_hbm, w_hbm, s_ref, ct_hbm, zt_hbm, lt_hbm, xf_hbm, xi_hbm,
    out_hbm, gin_hbm, wg_hbm,
    f_v, ct_v, o_v, gp_v, zt_v, lt_v, xf_v, xi_v, wl_v,
    sw, sa1, sd1, sa2, sd2, swg,
    ra1, rd1, ra2, rd2, rwg,
    wall, mall, ball,
    m_v, p_v, q_v, gx_v, e_v, wt_v, wo_v, ks_v, kb_v,
    lsem, ss, rs,
):
    me = lax.axis_index("gx")
    d = lax.axis_index("dp")
    bar = pltpu.get_barrier_semaphore()

    def greet_g(p, c):
        pl.semaphore_signal(bar, inc=1, device_id={"gx": lax.rem(me + p, GX)}, device_id_type=MESH)
        return c

    def greet_d(p, c):
        pl.semaphore_signal(bar, inc=1, device_id={"dp": lax.rem(d + p, DP)}, device_id_type=MESH)
        return c

    part, ih0, oh0 = d // 4, lax.rem(d // 2, 2), lax.rem(d, 2)
    w_copy = pltpu.make_async_copy(
        w_hbm.at[part, pl.ds(ih0 * 16, 16), pl.ds(oh0 * 16, 16), :], wl_v, lsem.at[0]
    )
    w_copy.start()
    zt_copy = pltpu.make_async_copy(zt_hbm, zt_v, lsem.at[1])
    zt_copy.start()
    f_copy = pltpu.make_async_copy(x_hbm, f_v, lsem.at[2])
    f_copy.start()
    lt_copy = pltpu.make_async_copy(lt_hbm, lt_v, lsem.at[3])
    lt_copy.start()
    xf_copy = pltpu.make_async_copy(xf_hbm, xf_v, lsem.at[4])
    xf_copy.start()
    xi_copy = pltpu.make_async_copy(xi_hbm, xi_v, lsem.at[5])
    xi_copy.start()
    ct_copy = pltpu.make_async_copy(ct_hbm, ct_v, lsem.at[6])
    ct_copy.start()
    lax.fori_loop(1, GX, greet_g, 0)
    lax.fori_loop(1, DP, greet_d, 0)

    def spread(send, recv, n):
        def body(p, c):
            t = lax.rem(me + p, GX)
            pltpu.make_async_remote_copy(
                send.at[t], recv.at[me], ss.at[n], rs.at[n],
                device_id={"gx": t}, device_id_type=MESH,
            ).start()
            return c

        lax.fori_loop(1, GX, body, 0)
        recv[me] = send[me]

    def wait_bytes(ref, sem, count):
        view = ref.at[pl.ds(0, count)]
        pltpu.make_async_copy(view, view, sem).wait()

    def share(buf, n):
        def body(p, c):
            pltpu.make_async_remote_copy(
                buf.at[d], buf.at[d], ss.at[n], rs.at[n],
                device_id={"dp": lax.rem(d + p, DP)}, device_id_type=MESH,
            ).start()
            return c

        lax.fori_loop(1, DP, body, 0)

    w_copy.wait()
    for kyh in range(2):
        wv = wl_v[:, :, kyh * 128:(kyh + 1) * 128].astype(F32)
        swapped = swap16(wv)
        for kz in range(16):
            sw[kyh * 16 + kz] = swapped[kz].astype(BF16)

    def planes(field, send):
        def body(t, acc):
            blocks = [
                field[x, pl.ds(t * 16, 16), h].reshape(256, 128)
                for h in range(2) for x in range(SLAB)
            ]
            fc = jnp.concatenate(blocks, axis=1)
            along_z = dot_nt(zt_v[...], fc).astype(BF16)
            return acc + dot(along_z, lt_v[pl.ds(pl.multiple_of(t * 256, 256), 256), :])

        u = lax.fori_loop(0, 4, body, jnp.zeros((256, 512), F32))
        u = u.reshape(16, 2, 8, 512)
        u0, u1 = u[:, 0], u[:, 1]
        re = u0[:, :, :256] - u1[:, :, 256:]
        im = u0[:, :, 256:] + u1[:, :, :256]
        both = jnp.stack([re, im], axis=1).reshape(16, 16, 256).astype(BF16)
        send[0:16] = both[:, :, :128]
        send[16:32] = both[:, :, 128:]

    zt_copy.wait()
    lt_copy.wait()
    f_copy.wait()
    planes(f_v, sa1)

    pl.semaphore_wait(bar, GX - 1 + DP - 1)

    def body_w(p, c):
        t = lax.rem(me + p, GX)
        pltpu.make_async_remote_copy(
            sw.at[t], wall.at[d, me], ss.at[0], rs.at[0],
            device_id={"gx": t}, device_id_type=MESH,
        ).start()
        return c

    lax.fori_loop(1, GX, body_w, 0)
    wall[d, me] = sw[me]
    spread(sa1, ra1, 1)

    er = iota((256, 32), 0)
    expand = (lax.rem(er, 32) == iota((256, 32), 1)).astype(F32).astype(BF16)
    same = iota((256, 256), 0) // 32 == iota((256, 256), 1) // 32
    sk = s_ref[...]
    es = dot(expand, sk).astype(BF16)
    kb_v[...] = jnp.where(same, dot_nt(es, expand), 0.0).astype(BF16)
    est = dot_nt(expand, sk).astype(BF16)
    ks_v[...] = jnp.where(same, dot_nt(est, expand), 0.0).astype(BF16)
    sum_l = (iota((64, 1024), 0) == iota((64, 1024), 1) // 16).astype(F32).astype(BF16)
    rep_l = (iota((1024, 64), 0) // 16 == iota((1024, 64), 1)).astype(F32).astype(BF16)
    ones_b = (iota((128, 128), 0) // 16 == iota((128, 128), 1) // 16).astype(F32).astype(BF16)
    diag = lax.rem(iota((1024, 128), 0), 16) == lax.rem(iota((1024, 128), 1), 16)

    wait_bytes(sw, rs.at[0], GX - 1)

    mate = d + 1 - 2 * lax.rem(d, 2)

    def body_x(p, c):
        pltpu.make_async_remote_copy(
            wall.at[d], wall.at[d], ss.at[2], rs.at[2],
            device_id={"dp": lax.rem(d + 2 * p, DP)}, device_id_type=MESH,
        ).start()
        return c

    lax.fori_loop(1, 4, body_x, 0)

    def body_c(p, c):
        slot = lax.rem(d + 2 * p, DP)
        pltpu.make_async_remote_copy(
            wall.at[slot], wall.at[slot], ss.at[3], rs.at[3],
            device_id={"dp": mate}, device_id_type=MESH,
        ).start()
        return c

    body_c(0, 0)

    def to_modes(recv, scale):
        r = recv[...].reshape(512, 128)
        return (dot(xf_v[...], r) * scale).astype(BF16)

    def to_slabs(mixed, send):
        send[...] = dot(xi_v[...], mixed).astype(BF16).reshape(PIECE)

    xf_copy.wait()
    xi_copy.wait()
    wait_bytes(ra1, rs.at[1], GX - 1)
    modes = to_modes(ra1, GRID_SCALE)
    mall[d] = modes
    share(mall, 4)
    m_v[...] = modes.astype(F32)

    wait_bytes(wall, rs.at[2], 3)
    lax.fori_loop(1, 4, body_c, 0)
    wait_bytes(wall, rs.at[3], 4)

    def weight(a, h, oh, k):
        return wall[4 * a + 2 * h + oh, k].astype(F32)

    def mix(k, c):
        mr = [m_v[pl.ds(h * 32 + k, 1), :] for h in range(2)]
        mi = [m_v[pl.ds(64 + h * 32 + k, 1), :] for h in range(2)]
        for oh in range(2):
            re = im = None
            for h in range(2):
                wr, wi = weight(0, h, oh, k), weight(1, h, oh, k)
                r = wr * mr[h] - wi * mi[h]
                i = wr * mi[h] + wi * mr[h]
                re = r if re is None else re + r
                im = i if im is None else im + i
            row = pl.multiple_of(oh * 512 + k * 16, 16)
            p_v[0, pl.ds(row, 16), :] = re.astype(BF16)
            p_v[1, pl.ds(row, 16), :] = im.astype(BF16)
        return c

    lax.fori_loop(0, MX, mix, 0)
    mixed = []
    for a in range(2):
        q = jnp.where(diag, dot(p_v[a], ones_b), 0.0).astype(BF16)
        mixed.append(dot(sum_l, q))
    to_slabs(jnp.concatenate(mixed, axis=0).astype(BF16), sd1)
    spread(sd1, rd1, 5)

    def unpack(recv):
        g = recv[...].astype(F32)
        g = jnp.concatenate([g[:16], g[16:]], axis=2).reshape(16, 2, 8, 256)
        turned = jnp.stack([g[:, 1], -g[:, 0]], axis=1).reshape(256, 256)
        gx_v[:, 0:256] = g.reshape(256, 256).astype(BF16)
        gx_v[:, 256:512] = turned.astype(BF16)

    def fields(scale, source, channel_map, emit):
        def body(t, c):
            lt_c = lt_v[pl.ds(pl.multiple_of(t * 128, 128), 128), :]
            vt = (dot_nt(lt_c, gx_v[...]) * scale).astype(BF16)
            for x in range(0, SLAB, 2):
                src = jnp.concatenate(
                    [source[x + i, pl.ds(t * 8, 8)].reshape(256, 128) for i in range(2)], axis=1
                )
                skip = dot(channel_map[...], src).reshape(8, 2, 16, 256)
                for h in range(2):
                    lo = (h * 4 + x) * 128
                    fld = dot(vt, zt_v[:, lo:lo + 256]).reshape(8, 16, 256)
                    total = fld + skip[:, h]
                    for i in range(2):
                        emit(x + i, t, h, total[:, :, i * 128:(i + 1) * 128])
            return c

        lax.fori_loop(0, 8, body, 0)

    ct_copy.wait()
    wait_bytes(rd1, rs.at[5], GX - 1)
    unpack(rd1)

    def emit_forward(x, t, h, pre):
        act, slope = gelu_pair(pre)
        ct = ct_v[x, pl.ds(t * 8, 8), h].astype(F32)
        o_v[x, pl.ds(t * 8, 8), h] = act.astype(BF16)
        gp_v[x, pl.ds(t * 8, 8), h] = (ct * slope).astype(BF16)

    fields(MODE_SCALE, f_v, ks_v, emit_forward)
    o_copy = pltpu.make_async_copy(o_v, out_hbm, lsem.at[7])
    o_copy.start()

    planes(gp_v, sa2)
    spread(sa2, ra2, 6)
    wait_bytes(ra2, rs.at[6], GX - 1)
    back = to_modes(ra2, MODE_SCALE)
    ball[d] = back
    share(ball, 7)

    for a in range(2):
        rows = jnp.where(diag, dot(rep_l, back[64 * a:64 * a + 64]), 0.0).astype(BF16)
        q_v[a] = dot(rows, ones_b)

    def conj_mix(k, c):
        for h in range(2):
            re = im = None
            for oh in range(2):
                row = pl.multiple_of(oh * 512 + k * 16, 16)
                br, bi = q_v[0, pl.ds(row, 16), :], q_v[1, pl.ds(row, 16), :]
                wr, wi = weight(0, h, oh, k), weight(1, h, oh, k)
                r = wr * br + wi * bi
                i = wr * bi - wi * br
                re = r if re is None else re + r
                im = i if im is None else im + i
            row = pl.multiple_of(h * 512 + k * 16, 16)
            p_v[0, pl.ds(row, 16), :] = re.astype(BF16)
            p_v[1, pl.ds(row, 16), :] = im.astype(BF16)
        return c

    lax.fori_loop(0, MX, conj_mix, 0)
    back_modes = [dot(sum_l, p_v[a]) for a in range(2)]
    to_slabs(jnp.concatenate(back_modes, axis=0).astype(BF16), sd2)
    spread(sd2, rd2, 8)

    wait_bytes(mall, rs.at[4], DP - 1)
    sel_r, sel_c = iota((128, 512), 0), iota((128, 512), 1)
    chan = 4 * lax.rem(d, 4) + sel_c // 128
    pick = (lax.rem(sel_r, 16) == chan) & (sel_r // 16 == lax.rem(sel_c, 128) // 16)
    pick = pick.astype(F32).astype(BF16)
    ihd = d // 4
    for a in range(2):
        start = pl.multiple_of(a * 64 + ihd * 32, 32)
        rows = mall[:, pl.ds(start, 32), :].reshape(256, 128)
        e_v[a] = dot(rows, pick)
    wait_bytes(ball, rs.at[7], DP - 1)
    for oh in range(2):
        for i4 in range(4):
            def add(n, acc):
                re, im = acc
                row = pl.multiple_of(n * 32, 32)
                er_ = e_v[0, pl.ds(row, 32), i4 * 128:(i4 + 1) * 128]
                ei_ = e_v[1, pl.ds(row, 32), i4 * 128:(i4 + 1) * 128]
                br = ball[n, oh * 32:oh * 32 + 32, :].astype(F32)
                bi = ball[n, 64 + oh * 32:64 + oh * 32 + 32, :].astype(F32)
                return re + er_ * br + ei_ * bi, im + er_ * bi - ei_ * br

            zero = jnp.zeros((32, 128), F32)
            re, im = lax.fori_loop(0, DP, add, (zero, zero))
            wt_v[:, i4 * 2 + oh, :] = re
            wt_v[:, 8 + i4 * 2 + oh, :] = im
    swg[...] = wt_v[...].astype(BF16)
    spread(swg, rwg, 9)

    wait_bytes(rd2, rs.at[8], GX - 1)
    unpack(rd2)
    o_copy.wait()

    def emit_backward(x, t, h, total):
        o_v[x, pl.ds(t * 8, 8), h] = total.astype(BF16)

    fields(GRID_SCALE, gp_v, kb_v, emit_backward)
    g_copy = pltpu.make_async_copy(o_v, gin_hbm, lsem.at[8])
    g_copy.start()

    wait_bytes(rwg, rs.at[9], GX - 1)
    for kyh in range(2):
        swapped = swap16(rwg[kyh * 16:kyh * 16 + 16].astype(F32))
        for o in range(16):
            wo_v[:, o, kyh * 128:(kyh + 1) * 128] = swapped[o]
    wg_copy = pltpu.make_async_copy(wo_v, wg_hbm, lsem.at[9])
    wg_copy.start()

    for n in (0, 1, 5, 6, 8, 9):
        wait_bytes(ra1, ss.at[n], GX - 1)
    wait_bytes(wall, ss.at[2], 3)
    wait_bytes(wall, ss.at[3], 4)
    wait_bytes(mall, ss.at[4], DP - 1)
    wait_bytes(ball, ss.at[7], DP - 1)
    g_copy.wait()
    wg_copy.wait()


def per_device(inputs, spectral_weights, skip_weights, cotangent, *tabs):
    shape5 = (SLAB, NY, 2, 16, NZ)
    any_spec = pl.BlockSpec(memory_space=pl.ANY)
    vm = pltpu.VMEM
    big = vm(shape5, BF16)
    piece = vm(PIECE, BF16)
    out, gin, wg = pl.pallas_call(
        kernel,
        out_shape=[
            jax.ShapeDtypeStruct(shape5, BF16),
            jax.ShapeDtypeStruct(shape5, BF16),
            jax.ShapeDtypeStruct((16, 16, 256), F32),
        ],
        in_specs=[any_spec, any_spec, pl.BlockSpec(memory_space=vm)] + [any_spec] * 5,
        out_specs=[any_spec] * 3,
        scratch_shapes=[
            big, big, big, big,
            vm((256, 1024), BF16), vm((1024, 512), BF16),
            vm((128, 512), BF16), vm((512, 128), BF16),
            vm((16, 16, 256), BF16),
            *([piece] * 11),
            vm((DP, *PIECE), BF16), vm((DP, 128, 128), BF16), vm((DP, 128, 128), BF16),
            vm((128, 128), F32), vm((2, 1024, 128), BF16), vm((2, 1024, 128), F32),
            vm((256, 512), BF16), vm((2, 256, 512), F32),
            vm(PIECE, F32), vm((16, 16, 256), F32),
            vm((256, 256), BF16), vm((256, 256), BF16),
            pltpu.SemaphoreType.DMA((10,)),
            pltpu.SemaphoreType.DMA((10,)),
            pltpu.SemaphoreType.DMA((10,)),
        ],
        compiler_params=pltpu.CompilerParams(
            collective_id=0, has_side_effects=True, vmem_limit_bytes=48 * 1024 * 1024
        ),
        cost_estimate=pl.CostEstimate(flops=8_000_000_000, bytes_accessed=12_000_000, transcendentals=1_048_576),
        name="spectral_layer",
    )(
        inputs.reshape(shape5), spectral_weights[0], skip_weights,
        cotangent.reshape(shape5), *tabs,
    )
    return (
        out.reshape(inputs.shape),
        gin.reshape(inputs.shape),
        wg.reshape(1, 2, 4, C, MY * MZ),
    )


def solution(mesh):
    field_spec = P("dp", "gx", None, None, None)
    in_specs = (field_spec, P("gx", None, None, None, None), P(), field_spec) + (P(),) * 4
    out_specs = (field_spec, field_spec, P("gx", None, "dp", None, None))
    mapped = jax.shard_map(
        per_device, mesh=mesh, in_specs=in_specs, out_specs=out_specs, check_vma=False
    )
    tabs = tables()

    def run(inputs, spectral_weights, skip_weights, cotangent):
        return mapped(
            inputs, spectral_weights, skip_weights, cotangent, *[jnp.asarray(t) for t in tabs]
        )

    return run
```

time: 1000 us -> 77.4 us (0.08)
  waiting for transfers between devices: 914 us -> 0 us
  Pallas kernels: 0 us -> 66.1 us
  matrix products: 31.5 us -> 0 us
  local copies, waits for them, and re-layouts: 29.5 us -> 10.3 us
  between operations: 14.7 us -> 0.66 us
    reduce_scatter x4 -> x0, waiting for transfers between devices: 861 us -> none  [the longest x2 437 us: to_slabs(): lax.psum_scatter(term(jnp.int32(0), slab_rows * lax.axis_size('gx')).asty...]
    pallas_call x0 -> x1, Pallas kernels: none -> 66.1 us  [per_device(): pl.pallas_call(kernel, out_shape=[jax.ShapeDtypeStruct(shape5, BF16), jax...]
    unnamed x6 -> x0, waiting for transfers between devices: 52.9 us -> none
    dot_general x14 -> x0, matrix products: 31.5 us -> none  [bdot(): return jnp.einsum(form, left, right, preferred_element_type=jnp.float32)]
    convert_element_type x4 -> x0, local copies, waits for them, and re-layouts: 11.8 us -> none  [the longest x2 8.73 us: to_slabs(): term(jnp.int32(0), slab_rows * lax.axis_size('gx')).astype(jnp.bfloat16)]
  transfers between devices with their start and end apart: 5 -> 0, of which waited for: 5 -> 0; matrix products, arithmetic and copies ran while one was open for 2% -> 0% of each run, Pallas kernels for 0% -> 0%
where the time goes in v1:
time: 77.4 us; the launch traced here: 77.1 us
  Pallas kernels  66.1 us (85%)
  local copies, waits for them, and re-layouts  10.3 us (13%)
    pallas_call x1, Pallas kernels, per_device(): pl.pallas_call(kernel, out_shape=[jax.ShapeDtypeStruct(shape5, BF16), jax...  66.1 us
    unnamed x17, local copies, waits for them, and re-layouts  10.3 us

profile of v1, /device:TPU:1, one launch (start us, length us, event | category | flops | bytes accessed | tf_op | source)
XLA Modules:
  0.0 77.1 jit_solution(15769393145436069838)
XLA Ops:
  0.6 0.0 copy-start
  0.6 1.2 %copy-done = bf16[1,2,32,32,256]{4,3,2,1,0:T(8,128)(2,1)S(1)} copy-done((bf16[1,2,32,32,256]{4,3,2,1,0:T(8,128)(2,1)S(1)}, bf16[1,2,32,32,256]{4,3,2,1,0:T(8,128)(2,1)}, u32[]{:S(2)}) %copy-start) | copy-done | bytes 1048600
  1.9 0.0 copy-start.1
  1.9 0.7 copy-done.1
  2.6 0.0 copy-start.2
  2.6 1.2 %copy-done.2 = bf16[1024,512]{1,0:T(8,128)(2,1)S(1)} copy-done((bf16[1024,512]{1,0:T(8,128)(2,1)S(1)}, bf16[1024,512]{1,0:T(8,128)(2,1)}, u32[]{:S(2)}) %copy-start.2) | copy-done | bytes 1048600
  3.8 0.0 copy-start.3
  3.8 1.0 %copy-done.3 = bf16[256,1024]{1,0:T(8,128)(2,1)S(1)} copy-done((bf16[256,1024]{1,0:T(8,128)(2,1)S(1)}, bf16[256,1024]{1,0:T(8,128)(2,1)}, u32[]{:S(2)}) %copy-start.3) | copy-done | bytes 524312
  4.8 0.0 copy-start.4
  4.8 0.9 %copy-done.4 = bf16[512,128]{1,0:T(8,128)(2,1)S(1)} copy-done((bf16[512,128]{1,0:T(8,128)(2,1)S(1)}, bf16[512,128]{1,0:T(8,128)(2,1)}, u32[]{:S(2)}) %copy-start.4) | copy-done | bytes 131096
  5.7 0.0 copy-start.5
  5.7 0.9 %copy-done.5 = bf16[128,512]{1,0:T(8,128)(2,1)S(1)} copy-done((bf16[128,512]{1,0:T(8,128)(2,1)S(1)}, bf16[128,512]{1,0:T(8,128)(2,1)}, u32[]{:S(2)}) %copy-start.5) | copy-done | bytes 131096
  6.6 66.1 %spectral_layer.1 = (bf16[4,64,2,16,128]{4,3,2,1,0:T(8,128)(2,1)S(1)}, bf16[4,64,2,16,128]{4,3,2,1,0:T(8,128)(2,1)}, f32[16,16,256]{2,1,0:T(8,128)S(1)}) custom-call(bf16[4,64,2,16,128]{4,3,2,1,0:T(8,128)(2,1)} %bitcast.10, bf16[2,32,32,256]{3,2,1,0:T(8,128)(2,1)S(1)} %bitcast.8, bf16[32,32]{1,0:T(8,128)(2,1)S(1)} %copy-done.1, ...), custom_call_target="tpu_custom_call" | custom-call | flops 8000000000 | bytes 12000000 | tf_op jit(solution)/shard_map/spectral_layer/pallas_call | solution.py:434
  72.7 0.0 copy-start.6
  72.7 1.3 %copy.14 = bf16[1,4,64,32,128]{4,3,2,1,0:T(8,128)(2,1)} copy(bf16[1,4,64,32,128]{4,3,2,1,0:T(8,128)(2,1)S(1)} %bitcast.6) | data formatting | bytes 4194304
  74.0 1.0 %copy-done.6 = bf16[4,64,2,16,128]{4,3,2,1,0:T(8,128)(2,1)S(1)} copy-done((bf16[4,64,2,16,128]{4,3,2,1,0:T(8,128)(2,1)S(1)}, bf16[4,64,2,16,128]{4,3,2,1,0:T(8,128)(2,1)}, u32[]{:S(2)}) %copy-start.6) | copy-done | bytes 2097176
  75.1 1.3 %copy.15 = bf16[1,4,64,32,128]{4,3,2,1,0:T(8,128)(2,1)} copy(bf16[1,4,64,32,128]{4,3,2,1,0:T(8,128)(2,1)S(1)} %bitcast.9) | data formatting | bytes 4194304
  76.4 0.7 copy.16
Async XLA Ops:
  0.6 1.2 %copy-start = (bf16[1,2,32,32,256]{4,3,2,1,0:T(8,128)(2,1)S(1)}, bf16[1,2,32,32,256]{4,3,2,1,0:T(8,128)(2,1)}, u32[]{:S(2)}) copy-start(bf16[1,2,32,32,256]{4,3,2,1,0:T(8,128)(2,1)} %param.9) | copy-start | bytes 3145732
  1.9 0.7 copy-start.1
  2.6 1.2 %copy-start.2 = (bf16[1024,512]{1,0:T(8,128)(2,1)S(1)}, bf16[1024,512]{1,0:T(8,128)(2,1)}, u32[]{:S(2)}) copy-start(bf16[1024,512]{1,0:T(8,128)(2,1)} %constant.9.clone.lt_hbm) | copy-start | bytes 3145732
  3.8 1.0 %copy-start.3 = (bf16[256,1024]{1,0:T(8,128)(2,1)S(1)}, bf16[256,1024]{1,0:T(8,128)(2,1)}, u32[]{:S(2)}) copy-start(bf16[256,1024]{1,0:T(8,128)(2,1)} %constant.8.clone.zt_hbm) | copy-start | bytes 1572868
  4.8 0.9 %copy-start.4 = (bf16[512,128]{1,0:T(8,128)(2,1)S(1)}, bf16[512,128]{1,0:T(8,128)(2,1)}, u32[]{:S(2)}) copy-start(bf16[512,128]{1,0:T(8,128)(2,1)} %constant.11.clone.xi_hbm) | copy-start | bytes 393220
  5.7 0.9 %copy-start.5 = (bf16[128,512]{1,0:T(8,128)(2,1)S(1)}, bf16[128,512]{1,0:T(8,128)(2,1)}, u32[]{:S(2)}) copy-start(bf16[128,512]{1,0:T(8,128)(2,1)} %constant.10.clone.xf_hbm) | copy-start | bytes 393220
  72.7 2.3 %copy-start.6 = (bf16[4,64,2,16,128]{4,3,2,1,0:T(8,128)(2,1)S(1)}, bf16[4,64,2,16,128]{4,3,2,1,0:T(8,128)(2,1)}, u32[]{:S(2)}) copy-start(bf16[4,64,2,16,128]{4,3,2,1,0:T(8,128)(2,1)} %get-tuple-element.7) | copy-start | bytes 6291460

commit v2 on v1

--- a/solution.py
+++ b/solution.py
@@ -20,6 +20,7 @@
 GRID_SCALE = 1.0 / math.sqrt(NX * NY * NZ)
 MODE_SCALE = 1.0 / math.sqrt(MX * MY * MZ)
 PIECE = (GX, 16, 128)
+ROUNDS = (3, 2, 1, 0)
 
 
 def angles(length, freqs):
@@ -50,6 +51,7 @@
     xf = xf.reshape(128, 512)
     return (
         zt.reshape(256, 1024).astype(bf),
+        np.ascontiguousarray(zt.reshape(256, 1024).T).astype(bf),
         lt.reshape(1024, 512).astype(bf),
         xf.astype(bf),
         np.ascontiguousarray(xf.T).astype(bf),
@@ -101,64 +103,80 @@
 
 
 def kernel(
-    x_hbm, w_hbm, s_ref, ct_hbm, zt_hbm, lt_hbm, xf_hbm, xi_hbm,
+    x_hbm, w_hbm, s_ref, ct_hbm, zt_hbm, zf_hbm, lt_hbm, xf_hbm, xi_hbm,
     out_hbm, gin_hbm, wg_hbm,
-    f_v, ct_v, o_v, gp_v, zt_v, lt_v, xf_v, xi_v, wl_v,
+    f_v, ct_v, o_v, gp_v, zt_v, zf_v, lt_v, xf_v, xi_v, wl_v,
     sw, sa1, sd1, sa2, sd2, swg,
     ra1, rd1, ra2, rd2, rwg,
     wall, mall, ball,
-    m_v, p_v, q_v, gx_v, e_v, wt_v, wo_v, ks_v, kb_v,
+    m_v, p_v, q_v, gx_v, e_v, sk_v, wt_v, wo_v, ks_v, kb_v,
     lsem, ss, rs,
 ):
     me = lax.axis_index("gx")
     d = lax.axis_index("dp")
     bar = pltpu.get_barrier_semaphore()
 
-    def greet_g(p, c):
-        pl.semaphore_signal(bar, inc=1, device_id={"gx": lax.rem(me + p, GX)}, device_id_type=MESH)
+    def peer(q):
+        i, j = q // 4, lax.rem(q, 4)
+        dz = 4 + (1 - 2 * lax.rem(i, 2)) * ((i + 1) // 2)
+        dy = 2 + (1 - 2 * lax.rem(j, 2)) * ((j + 1) // 2)
+        return lax.rem(me // 4 + dz, 8) * 4 + lax.rem(lax.rem(me, 4) + dy, 4)
+
+    def greet_g(q, c):
+        pl.semaphore_signal(bar, inc=1, device_id={"gx": peer(q)}, device_id_type=MESH)
         return c
 
     def greet_d(p, c):
         pl.semaphore_signal(bar, inc=1, device_id={"dp": lax.rem(d + p, DP)}, device_id_type=MESH)
         return c
 
+    lax.fori_loop(0, GX - 1, greet_g, 0, unroll=True)
+    lax.fori_loop(1, DP, greet_d, 0, unroll=True)
+
+    pending = {}
+
+    def load(name, src, dst, n):
+        copy = pltpu.make_async_copy(src, dst, lsem.at[n])
+        copy.start()
+        pending[name] = copy.wait
+
+    def settle(*names):
+        for name in names:
+            pending.pop(name)()
+
+    def wait_bytes(ref, sem, count):
+        view = ref.at[pl.ds(0, count)]
+        pltpu.make_async_copy(view, view, sem).wait()
+
+    def expect(name, n, ref, count):
+        pending[name] = lambda: wait_bytes(ref, rs.at[n], count)
+        pending[name + "_sent"] = lambda: wait_bytes(ref, ss.at[n], count)
+
     part, ih0, oh0 = d // 4, lax.rem(d // 2, 2), lax.rem(d, 2)
-    w_copy = pltpu.make_async_copy(
-        w_hbm.at[part, pl.ds(ih0 * 16, 16), pl.ds(oh0 * 16, 16), :], wl_v, lsem.at[0]
-    )
-    w_copy.start()
-    zt_copy = pltpu.make_async_copy(zt_hbm, zt_v, lsem.at[1])
-    zt_copy.start()
-    f_copy = pltpu.make_async_copy(x_hbm, f_v, lsem.at[2])
-    f_copy.start()
-    lt_copy = pltpu.make_async_copy(lt_hbm, lt_v, lsem.at[3])
-    lt_copy.start()
-    xf_copy = pltpu.make_async_copy(xf_hbm, xf_v, lsem.at[4])
-    xf_copy.start()
-    xi_copy = pltpu.make_async_copy(xi_hbm, xi_v, lsem.at[5])
-    xi_copy.start()
-    ct_copy = pltpu.make_async_copy(ct_hbm, ct_v, lsem.at[6])
-    ct_copy.start()
-    lax.fori_loop(1, GX, greet_g, 0)
-    lax.fori_loop(1, DP, greet_d, 0)
-
-    def spread(send, recv, n):
-        def body(p, c):
-            t = lax.rem(me + p, GX)
+    w_mine = w_hbm.at[part, pl.ds(ih0 * 16, 16), pl.ds(oh0 * 16, 16), :]
+    load("w", w_mine, wl_v, 0)
+    load("zf", zf_hbm, zf_v, 1)
+    load("f", x_hbm, f_v, 2)
+    load("lt", lt_hbm, lt_v, 3)
+    load("xf", xf_hbm, xf_v, 4)
+    load("xi", xi_hbm, xi_v, 5)
+    load("zt", zt_hbm, zt_v, 10)
+    load("ct", ct_hbm, ct_v, 6)
+
+    def spread(name, send, recv, n):
+        def body(q, c):
+            t = peer(q)
             pltpu.make_async_remote_copy(
                 send.at[t], recv.at[me], ss.at[n], rs.at[n],
                 device_id={"gx": t}, device_id_type=MESH,
             ).start()
             return c
 
-        lax.fori_loop(1, GX, body, 0)
+        lax.fori_loop(0, GX - 1, body, 0, unroll=True)
         recv[me] = send[me]
-
-    def wait_bytes(ref, sem, count):
-        view = ref.at[pl.ds(0, count)]
-        pltpu.make_async_copy(view, view, sem).wait()
-
-    def share(buf, n):
+        expect(name, n, recv, GX - 1)
+
+    def share(name, buf, n):
         def body(p, c):
             pltpu.make_async_remote_copy(
                 buf.at[d], buf.at[d], ss.at[n], rs.at[n],
@@ -166,9 +184,11 @@
             ).start()
             return c
 
-        lax.fori_loop(1, DP, body, 0)
-
-    w_copy.wait()
+        for p in (4, 5, 3, 6, 2, 7, 1):
+            body(p, 0)
+        expect(name, n, buf, DP - 1)
+
+    settle("w")
     for kyh in range(2):
         wv = wl_v[:, :, kyh * 128:(kyh + 1) * 128].astype(F32)
         swapped = swap16(wv)
@@ -182,7 +202,7 @@
                 for h in range(2) for x in range(SLAB)
             ]
             fc = jnp.concatenate(blocks, axis=1)
-            along_z = dot_nt(zt_v[...], fc).astype(BF16)
+            along_z = dot(fc, zf_v[...]).T.astype(BF16)
             return acc + dot(along_z, lt_v[pl.ds(pl.multiple_of(t * 256, 256), 256), :])
 
         u = lax.fori_loop(0, 4, body, jnp.zeros((256, 512), F32))
@@ -194,24 +214,27 @@
         send[0:16] = both[:, :, :128]
         send[16:32] = both[:, :, 128:]
 
-    zt_copy.wait()
-    lt_copy.wait()
-    f_copy.wait()
-    planes(f_v, sa1)
-
     pl.semaphore_wait(bar, GX - 1 + DP - 1)
 
-    def body_w(p, c):
-        t = lax.rem(me + p, GX)
+    def body_w(q, c):
+        t = peer(q)
         pltpu.make_async_remote_copy(
-            sw.at[t], wall.at[d, me], ss.at[0], rs.at[0],
+            sw.at[t], wall.at[d, me], ss.at[0], rs.at[20 + q // 8],
             device_id={"gx": t}, device_id_type=MESH,
         ).start()
         return c
 
-    lax.fori_loop(1, GX, body_w, 0)
+    for r in ROUNDS:
+        lax.fori_loop(8 * r, min(8 * r + 8, GX - 1), body_w, 0, unroll=True)
     wall[d, me] = sw[me]
-    spread(sa1, ra1, 1)
+    pending["weights_sent"] = lambda: wait_bytes(sw, ss.at[0], GX - 1)
+    for r in ROUNDS:
+        pending[f"weights_gx{r}"] = lambda r=r: wait_bytes(sw, rs.at[20 + r], min(8, GX - 1 - 8 * r))
+    settle("zf", "lt", "f")
+    planes(f_v, sa1)
+
+
+    spread("a1", sa1, ra1, 1)
 
     er = iota((256, 32), 0)
     expand = (lax.rem(er, 32) == iota((256, 32), 1)).astype(F32).astype(BF16)
@@ -226,28 +249,32 @@
     ones_b = (iota((128, 128), 0) // 16 == iota((128, 128), 1) // 16).astype(F32).astype(BF16)
     diag = lax.rem(iota((1024, 128), 0), 16) == lax.rem(iota((1024, 128), 1), 16)
 
-    wait_bytes(sw, rs.at[0], GX - 1)
-
     mate = d + 1 - 2 * lax.rem(d, 2)
 
-    def body_x(p, c):
-        pltpu.make_async_remote_copy(
-            wall.at[d], wall.at[d], ss.at[2], rs.at[2],
-            device_id={"dp": lax.rem(d + 2 * p, DP)}, device_id_type=MESH,
-        ).start()
-        return c
-
-    lax.fori_loop(1, 4, body_x, 0)
-
-    def body_c(p, c):
-        slot = lax.rem(d + 2 * p, DP)
-        pltpu.make_async_remote_copy(
-            wall.at[slot], wall.at[slot], ss.at[3], rs.at[3],
-            device_id={"dp": mate}, device_id_type=MESH,
-        ).start()
-        return c
-
-    body_c(0, 0)
+    def gather(slot, r, target, send_n, recv_n):
+        for i in (2 * r, 2 * r + 1):
+            dz = 4 + (1 - 2 * (i % 2)) * ((i + 1) // 2)
+            z = lax.rem(me // 4 + 8 - dz, 8)
+            block = wall.at[slot, pl.ds(4 * z, 4)]
+            pltpu.make_async_remote_copy(
+                block, block, ss.at[send_n], rs.at[recv_n],
+                device_id={"dp": target}, device_id_type=MESH,
+            ).start()
+
+    for r in ROUNDS:
+        settle(f"weights_gx{r}")
+        for p in (2, 1, 3):
+            gather(d, r, lax.rem(d + 2 * p, DP), 2, 24 + 3 * r + p - 1)
+        gather(d, r, mate, 3, 3)
+
+    def eight(sem):
+        view = wall.at[0, pl.ds(0, 8)]
+        pltpu.make_async_copy(view, view, sem).wait()
+
+    for r in ROUNDS:
+        for p in (1, 3, 2):
+            pending[f"weights_x{r}{p}"] = lambda n=24 + 3 * r + p - 1: eight(rs.at[n])
+    pending["weights_x_sent"] = lambda: wait_bytes(wall, ss.at[2], 3)
 
     def to_modes(recv, scale):
         r = recv[...].reshape(512, 128)
@@ -256,17 +283,17 @@
     def to_slabs(mixed, send):
         send[...] = dot(xi_v[...], mixed).astype(BF16).reshape(PIECE)
 
-    xf_copy.wait()
-    xi_copy.wait()
-    wait_bytes(ra1, rs.at[1], GX - 1)
+    settle("xf", "xi", "a1")
     modes = to_modes(ra1, GRID_SCALE)
     mall[d] = modes
-    share(mall, 4)
     m_v[...] = modes.astype(F32)
 
-    wait_bytes(wall, rs.at[2], 3)
-    lax.fori_loop(1, 4, body_c, 0)
-    wait_bytes(wall, rs.at[3], 4)
+    for r in ROUNDS:
+        for p in (1, 3, 2):
+            settle(f"weights_x{r}{p}")
+            gather(lax.rem(d + 8 - 2 * p, DP), r, mate, 3, 3)
+    expect("weights_core", 3, wall, 4)
+    settle("weights_core")
 
     def weight(a, h, oh, k):
         return wall[4 * a + 2 * h + oh, k].astype(F32)
@@ -287,42 +314,52 @@
             p_v[1, pl.ds(row, 16), :] = im.astype(BF16)
         return c
 
-    lax.fori_loop(0, MX, mix, 0)
+    lax.fori_loop(0, MX, mix, 0, unroll=4)
     mixed = []
     for a in range(2):
         q = jnp.where(diag, dot(p_v[a], ones_b), 0.0).astype(BF16)
         mixed.append(dot(sum_l, q))
     to_slabs(jnp.concatenate(mixed, axis=0).astype(BF16), sd1)
-    spread(sd1, rd1, 5)
+    spread("d1", sd1, rd1, 5)
 
     def unpack(recv):
         g = recv[...].astype(F32)
         g = jnp.concatenate([g[:16], g[16:]], axis=2).reshape(16, 2, 8, 256)
         turned = jnp.stack([g[:, 1], -g[:, 0]], axis=1).reshape(256, 256)
-        gx_v[:, 0:256] = g.reshape(256, 256).astype(BF16)
-        gx_v[:, 256:512] = turned.astype(BF16)
-
-    def fields(scale, source, channel_map, emit):
+        gx_v[0:256, :] = g.reshape(256, 256).T.astype(BF16)
+        gx_v[256:512, :] = turned.T.astype(BF16)
+
+    def skips(source, channel_map):
         def body(t, c):
-            lt_c = lt_v[pl.ds(pl.multiple_of(t * 128, 128), 128), :]
-            vt = (dot_nt(lt_c, gx_v[...]) * scale).astype(BF16)
             for x in range(0, SLAB, 2):
                 src = jnp.concatenate(
                     [source[x + i, pl.ds(t * 8, 8)].reshape(256, 128) for i in range(2)], axis=1
                 )
                 skip = dot(channel_map[...], src).reshape(8, 2, 16, 256)
+                for i in range(2):
+                    sk_v[x + i, pl.ds(t * 8, 8)] = skip[..., i * 128:(i + 1) * 128]
+            return c
+
+        lax.fori_loop(0, 8, body, 0)
+
+    def fields(scale, emit):
+        def body(t, c):
+            lt_c = lt_v[pl.ds(pl.multiple_of(t * 128, 128), 128), :]
+            vt = (dot(lt_c, gx_v[...]) * scale).astype(BF16)
+            for x in range(0, SLAB, 2):
                 for h in range(2):
                     lo = (h * 4 + x) * 128
                     fld = dot(vt, zt_v[:, lo:lo + 256]).reshape(8, 16, 256)
-                    total = fld + skip[:, h]
                     for i in range(2):
-                        emit(x + i, t, h, total[:, :, i * 128:(i + 1) * 128])
+                        skip = sk_v[x + i, pl.ds(t * 8, 8), h]
+                        emit(x + i, t, h, fld[:, :, i * 128:(i + 1) * 128] + skip)
             return c
 
         lax.fori_loop(0, 8, body, 0)
 
-    ct_copy.wait()
-    wait_bytes(rd1, rs.at[5], GX - 1)
+    share("mall", mall, 4)
+    skips(f_v, ks_v)
+    settle("ct", "zt", "d1")
     unpack(rd1)
 
     def emit_forward(x, t, h, pre):
@@ -331,16 +368,16 @@
         o_v[x, pl.ds(t * 8, 8), h] = act.astype(BF16)
         gp_v[x, pl.ds(t * 8, 8), h] = (ct * slope).astype(BF16)
 
-    fields(MODE_SCALE, f_v, ks_v, emit_forward)
-    o_copy = pltpu.make_async_copy(o_v, out_hbm, lsem.at[7])
-    o_copy.start()
+    fields(MODE_SCALE, emit_forward)
+    load("out", o_v, out_hbm, 7)
 
     planes(gp_v, sa2)
-    spread(sa2, ra2, 6)
-    wait_bytes(ra2, rs.at[6], GX - 1)
+    spread("a2", sa2, ra2, 6)
+    skips(gp_v, kb_v)
+    settle("a2")
     back = to_modes(ra2, MODE_SCALE)
     ball[d] = back
-    share(ball, 7)
+    share("ball", ball, 7)
 
     for a in range(2):
         rows = jnp.where(diag, dot(rep_l, back[64 * a:64 * a + 64]), 0.0).astype(BF16)
@@ -362,12 +399,12 @@
             p_v[1, pl.ds(row, 16), :] = im.astype(BF16)
         return c
 
-    lax.fori_loop(0, MX, conj_mix, 0)
+    lax.fori_loop(0, MX, conj_mix, 0, unroll=4)
     back_modes = [dot(sum_l, p_v[a]) for a in range(2)]
     to_slabs(jnp.concatenate(back_modes, axis=0).astype(BF16), sd2)
-    spread(sd2, rd2, 8)
-
-    wait_bytes(mall, rs.at[4], DP - 1)
+    spread("d2", sd2, rd2, 8)
+
+    settle("mall")
     sel_r, sel_c = iota((128, 512), 0), iota((128, 512), 1)
     chan = 4 * lax.rem(d, 4) + sel_c // 128
     pick = (lax.rem(sel_r, 16) == chan) & (sel_r // 16 == lax.rem(sel_c, 128) // 16)
@@ -377,7 +414,7 @@
         start = pl.multiple_of(a * 64 + ihd * 32, 32)
         rows = mall[:, pl.ds(start, 32), :].reshape(256, 128)
         e_v[a] = dot(rows, pick)
-    wait_bytes(ball, rs.at[7], DP - 1)
+    settle("ball")
     for oh in range(2):
         for i4 in range(4):
             def add(n, acc):
@@ -394,35 +431,34 @@
             wt_v[:, i4 * 2 + oh, :] = re
             wt_v[:, 8 + i4 * 2 + oh, :] = im
     swg[...] = wt_v[...].astype(BF16)
-    spread(swg, rwg, 9)
-
-    wait_bytes(rd2, rs.at[8], GX - 1)
+    spread("wg", swg, rwg, 9)
+
+    settle("d2", "out")
     unpack(rd2)
-    o_copy.wait()
 
     def emit_backward(x, t, h, total):
         o_v[x, pl.ds(t * 8, 8), h] = total.astype(BF16)
 
-    fields(GRID_SCALE, gp_v, kb_v, emit_backward)
-    g_copy = pltpu.make_async_copy(o_v, gin_hbm, lsem.at[8])
-    g_copy.start()
-
-    wait_bytes(rwg, rs.at[9], GX - 1)
+    fields(GRID_SCALE, emit_backward)
+    load("gin", o_v, gin_hbm, 8)
+
+    settle("wg")
     for kyh in range(2):
         swapped = swap16(rwg[kyh * 16:kyh * 16 + 16].astype(F32))
         for o in range(16):
             wo_v[:, o, kyh * 128:(kyh + 1) * 128] = swapped[o]
-    wg_copy = pltpu.make_async_copy(wo_v, wg_hbm, lsem.at[9])
-    wg_copy.start()
-
-    for n in (0, 1, 5, 6, 8, 9):
-        wait_bytes(ra1, ss.at[n], GX - 1)
-    wait_bytes(wall, ss.at[2], 3)
-    wait_bytes(wall, ss.at[3], 4)
-    wait_bytes(mall, ss.at[4], DP - 1)
-    wait_bytes(ball, ss.at[7], DP - 1)
-    g_copy.wait()
-    wg_copy.wait()
+    load("wg_out", wo_v, wg_hbm, 9)
+    settle(*list(pending))
+
+
+def writer(out_a, gin_a, wg_a, out_b, gin_b, wg_b, sem):
+    pairs = [(a.at[i], b.at[i]) for a, b in ((out_a, out_b), (gin_a, gin_b)) for i in range(SLAB)]
+    pairs.append((wg_a, wg_b))
+    copies = [pltpu.make_async_copy(a, b, sem.at[n]) for n, (a, b) in enumerate(pairs)]
+    for copy in copies:
+        copy.start()
+    for copy in copies:
+        copy.wait()
 
 
 def per_device(inputs, spectral_weights, skip_weights, cotangent, *tabs):
@@ -431,39 +467,51 @@
     vm = pltpu.VMEM
     big = vm(shape5, BF16)
     piece = vm(PIECE, BF16)
-    out, gin, wg = pl.pallas_call(
+    hbm = pl.BlockSpec(memory_space=pltpu.HBM)
+    keep = functools.partial(pltpu.with_memory_space_constraint, memory_space=pltpu.HBM)
+    shapes = [
+        jax.ShapeDtypeStruct(shape5, BF16),
+        jax.ShapeDtypeStruct(shape5, BF16),
+        jax.ShapeDtypeStruct((16, 16, 256), F32),
+    ]
+    results = pl.pallas_call(
         kernel,
-        out_shape=[
-            jax.ShapeDtypeStruct(shape5, BF16),
-            jax.ShapeDtypeStruct(shape5, BF16),
-            jax.ShapeDtypeStruct((16, 16, 256), F32),
-        ],
-        in_specs=[any_spec, any_spec, pl.BlockSpec(memory_space=vm)] + [any_spec] * 5,
+        out_shape=[vm(s.shape, s.dtype) for s in shapes],
+        in_specs=[hbm, hbm, pl.BlockSpec(memory_space=vm)] + [hbm] * 6,
         out_specs=[any_spec] * 3,
         scratch_shapes=[
             big, big, big, big,
-            vm((256, 1024), BF16), vm((1024, 512), BF16),
+            vm((256, 1024), BF16), vm((1024, 256), BF16), vm((1024, 512), BF16),
             vm((128, 512), BF16), vm((512, 128), BF16),
             vm((16, 16, 256), BF16),
             *([piece] * 11),
             vm((DP, *PIECE), BF16), vm((DP, 128, 128), BF16), vm((DP, 128, 128), BF16),
             vm((128, 128), F32), vm((2, 1024, 128), BF16), vm((2, 1024, 128), F32),
-            vm((256, 512), BF16), vm((2, 256, 512), F32),
+            vm((512, 256), BF16), vm((2, 256, 512), F32), vm(shape5, F32),
             vm(PIECE, F32), vm((16, 16, 256), F32),
             vm((256, 256), BF16), vm((256, 256), BF16),
-            pltpu.SemaphoreType.DMA((10,)),
-            pltpu.SemaphoreType.DMA((10,)),
-            pltpu.SemaphoreType.DMA((10,)),
+            pltpu.SemaphoreType.DMA((36,)),
+            pltpu.SemaphoreType.DMA((36,)),
+            pltpu.SemaphoreType.DMA((36,)),
         ],
         compiler_params=pltpu.CompilerParams(
-            collective_id=0, has_side_effects=True, vmem_limit_bytes=48 * 1024 * 1024
+            collective_id=0, has_side_effects=True, vmem_limit_bytes=40 * 1024 * 1024
         ),
         cost_estimate=pl.CostEstimate(flops=8_000_000_000, bytes_accessed=12_000_000, transcendentals=1_048_576),
         name="spectral_layer",
     )(
-        inputs.reshape(shape5), spectral_weights[0], skip_weights,
-        cotangent.reshape(shape5), *tabs,
+        keep(inputs.reshape(shape5)), keep(spectral_weights[0]), skip_weights,
+        keep(cotangent.reshape(shape5)), *map(keep, tabs),
     )
+    out, gin, wg = pl.pallas_call(
+        writer,
+        out_shape=shapes,
+        in_specs=[any_spec] * 3,
+        out_specs=[hbm] * 3,
+        scratch_shapes=[pltpu.SemaphoreType.DMA((9,))],
+        compiler_params=pltpu.CompilerParams(vmem_limit_bytes=1024 * 1024),
+        name="write_results",
+    )(*results)
     return (
         out.reshape(inputs.shape),
         gin.reshape(inputs.shape),
@@ -473,7 +521,7 @@
 
 def solution(mesh):
     field_spec = P("dp", "gx", None, None, None)
-    in_specs = (field_spec, P("gx", None, None, None, None), P(), field_spec) + (P(),) * 4
+    in_specs = (field_spec, P("gx", None, None, None, None), P(), field_spec) + (P(),) * 5
     out_specs = (field_spec, field_spec, P("gx", None, "dp", None, None))
     mapped = jax.shard_map(
         per_device, mesh=mesh, in_specs=in_specs, out_specs=out_specs, check_vma=False

time: 77.4 us -> 62 us (0.80)
  local copies, waits for them, and re-layouts: 10.3 us -> 0.69 us
  Pallas kernels: 66.1 us -> 60.5 us
    unnamed x17 -> x2, local copies, waits for them, and re-layouts: 10.3 us -> 0.69 us
    pallas_call x1 -> x2, Pallas kernels: 66.1 us -> 60.5 us  [the longest x1 58.4 us: per_device(): pl.pallas_call(kernel, out_shape=[vm(s.shape, s.dtype) for s in shapes],...]
where the time goes in v2:
time: 62 us; the launch traced here: 61.9 us
  Pallas kernels  60.5 us (98%)
  local copies, waits for them, and re-layouts  0.69 us (1%)
  between operations  0.65 us (1%)
    pallas_call x1, Pallas kernels, per_device(): pl.pallas_call(kernel, out_shape=[vm(s.shape, s.dtype) for s in shapes],...  58.4 us
    pallas_call x1, Pallas kernels, per_device(): pl.pallas_call(writer, out_shape=shapes, in_specs=[any_spec] * 3, out_spe...  2.16 us

profile of v2, /device:TPU:1, one launch (start us, length us, event | category | flops | bytes accessed | tf_op | source)
XLA Modules:
  0.0 61.9 jit_solution(9689691123655648354)
XLA Ops:
  0.6 0.0 copy-start
  0.6 0.7 %copy-done = bf16[32,32]{1,0:T(8,128)(2,1)S(1)} copy-done((bf16[32,32]{1,0:T(8,128)(2,1)S(1)}, bf16[32,32]{1,0:T(8,128)(2,1)}, u32[]{:S(2)}) %copy-start) | copy-done | bytes 2072
  1.3 58.4 %spectral_layer.1 = (bf16[4,64,2,16,128]{4,3,2,1,0:T(8,128)(2,1)S(1)}, bf16[4,64,2,16,128]{4,3,2,1,0:T(8,128)(2,1)S(1)}, f32[16,16,256]{2,1,0:T(8,128)S(1)}) custom-call(bf16[4,64,2,16,128]{4,3,2,1,0:T(8,128)(2,1)} %bitcast.6, bf16[2,32,32,256]{3,2,1,0:T(8,128)(2,1)} %bitcast.10, bf16[32,32]{1,0:T(8,128)(2,1)S(1)} %copy-done, ...), custom_call_target="tpu_custom_call" | custom-call | flops 8000000000 | bytes 12000000 | tf_op jit(solution)/shard_map/spectral_layer/pallas_call | solution.py:477
  59.7 2.2 %write_results.1 = (bf16[4,64,2,16,128]{4,3,2,1,0:T(8,128)(2,1)}, bf16[4,64,2,16,128]{4,3,2,1,0:T(8,128)(2,1)}, f32[16,16,256]{2,1,0:T(8,128)}) custom-call(bf16[4,64,2,16,128]{4,3,2,1,0:T(8,128)(2,1)S(1)} %get-tuple-element.9.out_a, bf16[4,64,2,16,128]{4,3,2,1,0:T(8,128)(2,1)S(1)} %get-tuple-element.10.gin_a, f32[16,16,256]{2,1,0:T(8,128)S(1)} %get-tuple-element.11.wg_a), custom_call_target="tpu_custom_call" | custom-call | tf_op jit(solution)/shard_map/write_results/pallas_call | solution.py:506
Async XLA Ops:
  0.6 0.7 %copy-start = (bf16[32,32]{1,0:T(8,128)(2,1)S(1)}, bf16[32,32]{1,0:T(8,128)(2,1)}, u32[]{:S(2)}) copy-start(bf16[32,32]{1,0:T(8,128)(2,1)} %s_ref.1) | copy-start | bytes 6148

commit v3 on v2

--- a/solution.py
+++ b/solution.py
@@ -95,21 +95,21 @@
 
 def gelu_pair(x):
     k0 = math.sqrt(2.0 / math.pi)
-    x2 = x * x
-    t = jnp.tanh(k0 * (x + 0.044715 * (x2 * x)))
-    half = 0.5 * (1.0 + t)
-    slope = half + (0.5 * k0) * x * (1.0 - t * t) * (1.0 + (3.0 * 0.044715) * x2)
+    u = x * (k0 + (k0 * 0.044715) * (x * x))
+    t = jnp.tanh(u)
+    half = 0.5 * t + 0.5
+    slope = half + (1.5 * u - k0 * x) * (1.0 - t * t)
     return x * half, slope
 
 
 def kernel(
-    x_hbm, w_hbm, s_ref, ct_hbm, zt_hbm, zf_hbm, lt_hbm, xf_hbm, xi_hbm,
+    x_hbm, w_hbm, s_hbm, ct_hbm, zt_hbm, zf_hbm, lt_hbm, xf_hbm, xi_hbm,
     out_hbm, gin_hbm, wg_hbm,
     f_v, ct_v, o_v, gp_v, zt_v, zf_v, lt_v, xf_v, xi_v, wl_v,
     sw, sa1, sd1, sa2, sd2, swg,
     ra1, rd1, ra2, rd2, rwg,
     wall, mall, ball,
-    m_v, p_v, q_v, gx_v, e_v, sk_v, wt_v, wo_v, ks_v, kb_v,
+    m_v, p_v, q_v, gx_v, e_v, sk_v, t_v, sk_w, wt_v, wo_v, ks_v, kb_v,
     lsem, ss, rs,
 ):
     me = lax.axis_index("gx")
@@ -152,12 +152,15 @@
         pending[name] = lambda: wait_bytes(ref, rs.at[n], count)
         pending[name + "_sent"] = lambda: wait_bytes(ref, ss.at[n], count)
 
-    part, ih0, oh0 = d // 4, lax.rem(d // 2, 2), lax.rem(d, 2)
-    w_mine = w_hbm.at[part, pl.ds(ih0 * 16, 16), pl.ds(oh0 * 16, 16), :]
+    ih0, oh0 = lax.rem(d // 2, 2), lax.rem(d, 2)
+    slot = 2 * ih0 + oh0
+    other = lax.rem(slot + 2, 4)
+    w_mine = w_hbm.at[:, pl.ds(ih0 * 16, 16), pl.ds(oh0 * 16, 16), :]
     load("w", w_mine, wl_v, 0)
     load("zf", zf_hbm, zf_v, 1)
     load("f", x_hbm, f_v, 2)
     load("lt", lt_hbm, lt_v, 3)
+    load("s", s_hbm, sk_w, 11)
     load("xf", xf_hbm, xf_v, 4)
     load("xi", xi_hbm, xi_v, 5)
     load("zt", zt_hbm, zt_v, 10)
@@ -189,23 +192,21 @@
         expect(name, n, buf, DP - 1)
 
     settle("w")
-    for kyh in range(2):
-        wv = wl_v[:, :, kyh * 128:(kyh + 1) * 128].astype(F32)
-        swapped = swap16(wv)
-        for kz in range(16):
-            sw[kyh * 16 + kz] = swapped[kz].astype(BF16)
+    for a in range(2):
+        for kyh in range(2):
+            swapped = swap16(wl_v[a, :, :, kyh * 128:(kyh + 1) * 128].astype(F32))
+            for kz in range(16):
+                sw[kyh * 16 + kz, a] = swapped[kz].astype(BF16)
 
     def planes(field, send):
-        def body(t, acc):
+        for t in range(4):
             blocks = [
                 field[x, pl.ds(t * 16, 16), h].reshape(256, 128)
                 for h in range(2) for x in range(SLAB)
             ]
-            fc = jnp.concatenate(blocks, axis=1)
-            along_z = dot(fc, zf_v[...]).T.astype(BF16)
-            return acc + dot(along_z, lt_v[pl.ds(pl.multiple_of(t * 256, 256), 256), :])
-
-        u = lax.fori_loop(0, 4, body, jnp.zeros((256, 512), F32))
+            along_z = dot(jnp.concatenate(blocks, axis=1), zf_v[...])
+            t_v[:, t * 256:(t + 1) * 256] = along_z.T.astype(BF16)
+        u = dot(t_v[...], lt_v[...])
         u = u.reshape(16, 2, 8, 512)
         u0, u1 = u[:, 0], u[:, 1]
         re = u0[:, :, :256] - u1[:, :, 256:]
@@ -214,32 +215,14 @@
         send[0:16] = both[:, :, :128]
         send[16:32] = both[:, :, 128:]
 
-    pl.semaphore_wait(bar, GX - 1 + DP - 1)
-
-    def body_w(q, c):
-        t = peer(q)
-        pltpu.make_async_remote_copy(
-            sw.at[t], wall.at[d, me], ss.at[0], rs.at[20 + q // 8],
-            device_id={"gx": t}, device_id_type=MESH,
-        ).start()
-        return c
-
-    for r in ROUNDS:
-        lax.fori_loop(8 * r, min(8 * r + 8, GX - 1), body_w, 0, unroll=True)
-    wall[d, me] = sw[me]
-    pending["weights_sent"] = lambda: wait_bytes(sw, ss.at[0], GX - 1)
-    for r in ROUNDS:
-        pending[f"weights_gx{r}"] = lambda r=r: wait_bytes(sw, rs.at[20 + r], min(8, GX - 1 - 8 * r))
     settle("zf", "lt", "f")
     planes(f_v, sa1)
-
-
-    spread("a1", sa1, ra1, 1)
 
     er = iota((256, 32), 0)
     expand = (lax.rem(er, 32) == iota((256, 32), 1)).astype(F32).astype(BF16)
     same = iota((256, 256), 0) // 32 == iota((256, 256), 1) // 32
-    sk = s_ref[...]
+    settle("s")
+    sk = sk_w[...]
     es = dot(expand, sk).astype(BF16)
     kb_v[...] = jnp.where(same, dot_nt(es, expand), 0.0).astype(BF16)
     est = dot_nt(expand, sk).astype(BF16)
@@ -249,32 +232,58 @@
     ones_b = (iota((128, 128), 0) // 16 == iota((128, 128), 1) // 16).astype(F32).astype(BF16)
     diag = lax.rem(iota((1024, 128), 0), 16) == lax.rem(iota((1024, 128), 1), 16)
 
+
+    pl.semaphore_wait(bar, GX - 1 + DP - 1)
+
+    def body_w(q, c):
+        t = peer(q)
+        pltpu.make_async_remote_copy(
+            sw.at[t], wall.at[slot, me], ss.at[0], rs.at[20 + q // 8],
+            device_id={"gx": t}, device_id_type=MESH,
+        ).start()
+        return c
+
+    for r in ROUNDS:
+        lax.fori_loop(8 * r, min(8 * r + 8, GX - 1), body_w, 0, unroll=True)
+    wall[slot, me] = sw[me]
+    pending["weights_sent"] = lambda: wait_bytes(sw, ss.at[0], GX - 1)
+    for r in ROUNDS:
+        pending[f"weights_gx{r}"] = lambda r=r: wait_bytes(sw, rs.at[20 + r], min(8, GX - 1 - 8 * r))
+    spread("a1", sa1, ra1, 1)
+
     mate = d + 1 - 2 * lax.rem(d, 2)
 
-    def gather(slot, r, target, send_n, recv_n):
-        for i in (2 * r, 2 * r + 1):
-            dz = 4 + (1 - 2 * (i % 2)) * ((i + 1) // 2)
-            z = lax.rem(me // 4 + 8 - dz, 8)
-            block = wall.at[slot, pl.ds(4 * z, 4)]
-            pltpu.make_async_remote_copy(
-                block, block, ss.at[send_n], rs.at[recv_n],
-                device_id={"dp": target}, device_id_type=MESH,
-            ).start()
+    def gather(s, i, target, send_n, recv_n):
+        dz = 4 + (1 - 2 * (i % 2)) * ((i + 1) // 2)
+        z = lax.rem(me // 4 + 8 - dz, 8)
+        block = wall.at[s, pl.ds(4 * z, 4)]
+        pltpu.make_async_remote_copy(
+            block, block, ss.at[send_n], rs.at[recv_n],
+            device_id={"dp": target}, device_id_type=MESH,
+        ).start()
 
     for r in ROUNDS:
         settle(f"weights_gx{r}")
-        for p in (2, 1, 3):
-            gather(d, r, lax.rem(d + 2 * p, DP), 2, 24 + 3 * r + p - 1)
-        gather(d, r, mate, 3, 3)
-
-    def eight(sem):
-        view = wall.at[0, pl.ds(0, 8)]
+        gather(slot, 2 * r, lax.rem(d + 2, DP), 2, 24 + 2 * r)
+        gather(slot, 2 * r + 1, lax.rem(d + 6, DP), 2, 25 + 2 * r)
+        for i in (2 * r, 2 * r + 1):
+            gather(slot, i, mate, 3, 3)
+
+    def four(sem):
+        view = wall.at[0, pl.ds(0, 4)]
         pltpu.make_async_copy(view, view, sem).wait()
 
-    for r in ROUNDS:
-        for p in (1, 3, 2):
-            pending[f"weights_x{r}{p}"] = lambda n=24 + 3 * r + p - 1: eight(rs.at[n])
-    pending["weights_x_sent"] = lambda: wait_bytes(wall, ss.at[2], 3)
+    for i in range(8):
+        pending[f"weights_x{i}"] = lambda i=i: four(rs.at[24 + i])
+    pending["weights_x_sent"] = lambda: wait_bytes(wall, ss.at[2], 1)
+
+    def pass_on(rounds):
+        for r in rounds:
+            for i in (2 * r, 2 * r + 1):
+                settle(f"weights_x{i}")
+                gather(other, i, mate, 3, 3)
+
+    pass_on(ROUNDS[:2])
 
     def to_modes(recv, scale):
         r = recv[...].reshape(512, 128)
@@ -288,15 +297,12 @@
     mall[d] = modes
     m_v[...] = modes.astype(F32)
 
-    for r in ROUNDS:
-        for p in (1, 3, 2):
-            settle(f"weights_x{r}{p}")
-            gather(lax.rem(d + 8 - 2 * p, DP), r, mate, 3, 3)
-    expect("weights_core", 3, wall, 4)
+    pass_on(ROUNDS[2:])
+    expect("weights_core", 3, wall, 2)
     settle("weights_core")
 
     def weight(a, h, oh, k):
-        return wall[4 * a + 2 * h + oh, k].astype(F32)
+        return wall[2 * h + oh, k, a].astype(F32)
 
     def mix(k, c):
         mr = [m_v[pl.ds(h * 32 + k, 1), :] for h in range(2)]
@@ -314,7 +320,7 @@
             p_v[1, pl.ds(row, 16), :] = im.astype(BF16)
         return c
 
-    lax.fori_loop(0, MX, mix, 0, unroll=4)
+    lax.fori_loop(0, MX, mix, 0, unroll=8)
     mixed = []
     for a in range(2):
         q = jnp.where(diag, dot(p_v[a], ones_b), 0.0).astype(BF16)
@@ -343,30 +349,26 @@
         lax.fori_loop(0, 8, body, 0)
 
     def fields(scale, emit):
-        def body(t, c):
-            lt_c = lt_v[pl.ds(pl.multiple_of(t * 128, 128), 128), :]
-            vt = (dot(lt_c, gx_v[...]) * scale).astype(BF16)
+        for t in range(4):
+            vt = (dot(lt_v[t * 256:(t + 1) * 256, :], gx_v[...]) * scale).astype(BF16)
             for x in range(0, SLAB, 2):
                 for h in range(2):
                     lo = (h * 4 + x) * 128
-                    fld = dot(vt, zt_v[:, lo:lo + 256]).reshape(8, 16, 256)
+                    fld = dot(vt, zt_v[:, lo:lo + 256]).reshape(16, 16, 256)
                     for i in range(2):
-                        skip = sk_v[x + i, pl.ds(t * 8, 8), h]
-                        emit(x + i, t, h, fld[:, :, i * 128:(i + 1) * 128] + skip)
-            return c
-
-        lax.fori_loop(0, 8, body, 0)
+                        rows = pl.ds(t * 16, 16)
+                        total = fld[:, :, i * 128:(i + 1) * 128] + sk_v[x + i, rows, h]
+                        emit(x + i, rows, h, total)
 
     share("mall", mall, 4)
     skips(f_v, ks_v)
     settle("ct", "zt", "d1")
     unpack(rd1)
 
-    def emit_forward(x, t, h, pre):
+    def emit_forward(x, rows, h, pre):
         act, slope = gelu_pair(pre)
-        ct = ct_v[x, pl.ds(t * 8, 8), h].astype(F32)
-        o_v[x, pl.ds(t * 8, 8), h] = act.astype(BF16)
-        gp_v[x, pl.ds(t * 8, 8), h] = (ct * slope).astype(BF16)
+        o_v[x, rows, h] = act.astype(BF16)
+        gp_v[x, rows, h] = (ct_v[x, rows, h].astype(F32) * slope).astype(BF16)
 
     fields(MODE_SCALE, emit_forward)
     load("out", o_v, out_hbm, 7)
@@ -399,7 +401,7 @@
             p_v[1, pl.ds(row, 16), :] = im.astype(BF16)
         return c
 
-    lax.fori_loop(0, MX, conj_mix, 0, unroll=4)
+    lax.fori_loop(0, MX, conj_mix, 0, unroll=8)
     back_modes = [dot(sum_l, p_v[a]) for a in range(2)]
     to_slabs(jnp.concatenate(back_modes, axis=0).astype(BF16), sd2)
     spread("d2", sd2, rd2, 8)
@@ -427,7 +429,7 @@
                 return re + er_ * br + ei_ * bi, im + er_ * bi - ei_ * br
 
             zero = jnp.zeros((32, 128), F32)
-            re, im = lax.fori_loop(0, DP, add, (zero, zero))
+            re, im = lax.fori_loop(0, DP, add, (zero, zero), unroll=True)
             wt_v[:, i4 * 2 + oh, :] = re
             wt_v[:, 8 + i4 * 2 + oh, :] = im
     swg[...] = wt_v[...].astype(BF16)
@@ -436,8 +438,8 @@
     settle("d2", "out")
     unpack(rd2)
 
-    def emit_backward(x, t, h, total):
-        o_v[x, pl.ds(t * 8, 8), h] = total.astype(BF16)
+    def emit_backward(x, rows, h, total):
+        o_v[x, rows, h] = total.astype(BF16)
 
     fields(GRID_SCALE, emit_backward)
     load("gin", o_v, gin_hbm, 8)
@@ -477,17 +479,17 @@
     results = pl.pallas_call(
         kernel,
         out_shape=[vm(s.shape, s.dtype) for s in shapes],
-        in_specs=[hbm, hbm, pl.BlockSpec(memory_space=vm)] + [hbm] * 6,
+        in_specs=[hbm] * 9,
         out_specs=[any_spec] * 3,
         scratch_shapes=[
             big, big, big, big,
             vm((256, 1024), BF16), vm((1024, 256), BF16), vm((1024, 512), BF16),
             vm((128, 512), BF16), vm((512, 128), BF16),
-            vm((16, 16, 256), BF16),
-            *([piece] * 11),
-            vm((DP, *PIECE), BF16), vm((DP, 128, 128), BF16), vm((DP, 128, 128), BF16),
+            vm((2, 16, 16, 256), BF16),
+            vm((GX, 2, 16, 128), BF16), *([piece] * 10),
+            vm((4, GX, 2, 16, 128), BF16), vm((DP, 128, 128), BF16), vm((DP, 128, 128), BF16),
             vm((128, 128), F32), vm((2, 1024, 128), BF16), vm((2, 1024, 128), F32),
-            vm((512, 256), BF16), vm((2, 256, 512), F32), vm(shape5, F32),
+            vm((512, 256), BF16), vm((2, 256, 512), F32), vm(shape5, F32), vm((256, 1024), BF16), vm((32, 32), BF16),
             vm(PIECE, F32), vm((16, 16, 256), F32),
             vm((256, 256), BF16), vm((256, 256), BF16),
             pltpu.SemaphoreType.DMA((36,)),
@@ -500,7 +502,7 @@
         cost_estimate=pl.CostEstimate(flops=8_000_000_000, bytes_accessed=12_000_000, transcendentals=1_048_576),
         name="spectral_layer",
     )(
-        keep(inputs.reshape(shape5)), keep(spectral_weights[0]), skip_weights,
+        keep(inputs.reshape(shape5)), keep(spectral_weights[0]), keep(skip_weights),
         keep(cotangent.reshape(shape5)), *map(keep, tabs),
     )
     out, gin, wg = pl.pallas_call(

time: 62 us -> 59.8 us (0.965)
  Pallas kernels: 60.5 us -> 59.1 us
  local copies, waits for them, and re-layouts: 0.69 us -> 0 us
    pallas_call x1, Pallas kernels: 58.4 us -> 56.9 us  [per_device(): pl.pallas_call(kernel, out_shape=[vm(s.shape, s.dtype) for s in shapes],...]
    unnamed x2 -> x0, local copies, waits for them, and re-layouts: 0.69 us -> none
where the time goes in v3:
time: 59.8 us; the launch traced here: 59.7 us
  Pallas kernels  59.1 us (99%)
  between operations  0.64 us (1%)
    pallas_call x1, Pallas kernels, per_device(): pl.pallas_call(kernel, out_shape=[vm(s.shape, s.dtype) for s in shapes],...  56.9 us
    pallas_call x1, Pallas kernels, per_device(): pl.pallas_call(writer, out_shape=shapes, in_specs=[any_spec] * 3, out_spe...  2.16 us

profile of v3, /device:TPU:1, one launch (start us, length us, event | category | flops | bytes accessed | tf_op | source)
XLA Modules:
  0.0 59.7 jit_solution(3134840979381834669)
XLA Ops:
  0.6 56.9 %spectral_layer.1 = (bf16[4,64,2,16,128]{4,3,2,1,0:T(8,128)(2,1)S(1)}, bf16[4,64,2,16,128]{4,3,2,1,0:T(8,128)(2,1)S(1)}, f32[16,16,256]{2,1,0:T(8,128)S(1)}) custom-call(bf16[4,64,2,16,128]{4,3,2,1,0:T(8,128)(2,1)} %bitcast.6, bf16[2,32,32,256]{3,2,1,0:T(8,128)(2,1)} %bitcast.10, bf16[32,32]{1,0:T(8,128)(2,1)} %s_hbm.1, ...), custom_call_target="tpu_custom_call" | custom-call | flops 8000000000 | bytes 12000000 | tf_op jit(solution)/shard_map/spectral_layer/pallas_call | solution.py:479
  57.6 2.2 %write_results.1 = (bf16[4,64,2,16,128]{4,3,2,1,0:T(8,128)(2,1)}, bf16[4,64,2,16,128]{4,3,2,1,0:T(8,128)(2,1)}, f32[16,16,256]{2,1,0:T(8,128)}) custom-call(bf16[4,64,2,16,128]{4,3,2,1,0:T(8,128)(2,1)S(1)} %get-tuple-element.9.out_a, bf16[4,64,2,16,128]{4,3,2,1,0:T(8,128)(2,1)S(1)} %get-tuple-element.10.gin_a, f32[16,16,256]{2,1,0:T(8,128)S(1)} %get-tuple-element.11.wg_a), custom_call_target="tpu_custom_call" | custom-call | tf_op jit(solution)/shard_map/write_results/pallas_call | solution.py:508

commit v4 on v3

--- a/solution.py
+++ b/solution.py
@@ -109,7 +109,7 @@
     sw, sa1, sd1, sa2, sd2, swg,
     ra1, rd1, ra2, rd2, rwg,
     wall, mall, ball,
-    m_v, p_v, q_v, gx_v, e_v, sk_v, t_v, sk_w, wt_v, wo_v, ks_v, kb_v,
+    m_v, p_v, q_v, gx_v, e_v, sk_v, t_v, sk_w, wt_v, ks_v, kb_v,
     lsem, ss, rs,
 ):
     me = lax.axis_index("gx")
@@ -130,9 +130,6 @@
         pl.semaphore_signal(bar, inc=1, device_id={"dp": lax.rem(d + p, DP)}, device_id_type=MESH)
         return c
 
-    lax.fori_loop(0, GX - 1, greet_g, 0, unroll=True)
-    lax.fori_loop(1, DP, greet_d, 0, unroll=True)
-
     pending = {}
 
     def load(name, src, dst, n):
@@ -152,11 +149,11 @@
         pending[name] = lambda: wait_bytes(ref, rs.at[n], count)
         pending[name + "_sent"] = lambda: wait_bytes(ref, ss.at[n], count)
 
-    ih0, oh0 = lax.rem(d // 2, 2), lax.rem(d, 2)
-    slot = 2 * ih0 + oh0
-    other = lax.rem(slot + 2, 4)
-    w_mine = w_hbm.at[:, pl.ds(ih0 * 16, 16), pl.ds(oh0 * 16, 16), :]
+    part, ih0, oh0 = d // 4, lax.rem(d // 2, 2), lax.rem(d, 2)
+    w_mine = w_hbm.at[part, pl.ds(ih0 * 16, 16), pl.ds(oh0 * 16, 16), :]
     load("w", w_mine, wl_v, 0)
+    lax.fori_loop(0, GX - 1, greet_g, 0, unroll=True)
+    lax.fori_loop(1, DP, greet_d, 0, unroll=True)
     load("zf", zf_hbm, zf_v, 1)
     load("f", x_hbm, f_v, 2)
     load("lt", lt_hbm, lt_v, 3)
@@ -192,11 +189,10 @@
         expect(name, n, buf, DP - 1)
 
     settle("w")
-    for a in range(2):
-        for kyh in range(2):
-            swapped = swap16(wl_v[a, :, :, kyh * 128:(kyh + 1) * 128].astype(F32))
-            for kz in range(16):
-                sw[kyh * 16 + kz, a] = swapped[kz].astype(BF16)
+    for kyh in range(2):
+        swapped = swap16(wl_v[:, :, kyh * 128:(kyh + 1) * 128].astype(F32))
+        for kz in range(16):
+            sw[kyh * 16 + kz] = swapped[kz].astype(BF16)
 
     def planes(field, send):
         for t in range(4):
@@ -215,8 +211,25 @@
         send[0:16] = both[:, :, :128]
         send[16:32] = both[:, :, 128:]
 
+    pl.semaphore_wait(bar, GX - 1 + DP - 1)
+
+    def body_w(q, c):
+        t = peer(q)
+        pltpu.make_async_remote_copy(
+            sw.at[t], wall.at[d, me], ss.at[0], rs.at[20 + q // 8],
+            device_id={"gx": t}, device_id_type=MESH,
+        ).start()
+        return c
+
+    for r in ROUNDS:
+        lax.fori_loop(8 * r, min(8 * r + 8, GX - 1), body_w, 0, unroll=True)
+    wall[d, me] = sw[me]
+    pending["weights_sent"] = lambda: wait_bytes(sw, ss.at[0], GX - 1)
+    for r in ROUNDS:
+        pending[f"weights_gx{r}"] = lambda r=r: wait_bytes(sw, rs.at[20 + r], min(8, GX - 1 - 8 * r))
     settle("zf", "lt", "f")
     planes(f_v, sa1)
+    spread("a1", sa1, ra1, 1)
 
     er = iota((256, 32), 0)
     expand = (lax.rem(er, 32) == iota((256, 32), 1)).astype(F32).astype(BF16)
@@ -233,29 +246,13 @@
     diag = lax.rem(iota((1024, 128), 0), 16) == lax.rem(iota((1024, 128), 1), 16)
 
 
-    pl.semaphore_wait(bar, GX - 1 + DP - 1)
-
-    def body_w(q, c):
-        t = peer(q)
-        pltpu.make_async_remote_copy(
-            sw.at[t], wall.at[slot, me], ss.at[0], rs.at[20 + q // 8],
-            device_id={"gx": t}, device_id_type=MESH,
-        ).start()
-        return c
-
-    for r in ROUNDS:
-        lax.fori_loop(8 * r, min(8 * r + 8, GX - 1), body_w, 0, unroll=True)
-    wall[slot, me] = sw[me]
-    pending["weights_sent"] = lambda: wait_bytes(sw, ss.at[0], GX - 1)
-    for r in ROUNDS:
-        pending[f"weights_gx{r}"] = lambda r=r: wait_bytes(sw, rs.at[20 + r], min(8, GX - 1 - 8 * r))
-    spread("a1", sa1, ra1, 1)
-
     mate = d + 1 - 2 * lax.rem(d, 2)
 
+    def block_z(i):
+        return lax.rem(me // 4 + 4 - (1 - 2 * (i % 2)) * ((i + 1) // 2), 8)
+
     def gather(s, i, target, send_n, recv_n):
-        dz = 4 + (1 - 2 * (i % 2)) * ((i + 1) // 2)
-        z = lax.rem(me // 4 + 8 - dz, 8)
+        z = block_z(i)
         block = wall.at[s, pl.ds(4 * z, 4)]
         pltpu.make_async_remote_copy(
             block, block, ss.at[send_n], rs.at[recv_n],
@@ -264,26 +261,23 @@
 
     for r in ROUNDS:
         settle(f"weights_gx{r}")
-        gather(slot, 2 * r, lax.rem(d + 2, DP), 2, 24 + 2 * r)
-        gather(slot, 2 * r + 1, lax.rem(d + 6, DP), 2, 25 + 2 * r)
+        for p in (2, 1, 3):
+            for i in (2 * r, 2 * r + 1):
+                gather(d, i, lax.rem(d + 2 * p, DP), 2, 24 + 3 * r + p - 1)
         for i in (2 * r, 2 * r + 1):
-            gather(slot, i, mate, 3, 3)
-
-    def four(sem):
-        view = wall.at[0, pl.ds(0, 4)]
-        pltpu.make_async_copy(view, view, sem).wait()
-
-    for i in range(8):
-        pending[f"weights_x{i}"] = lambda i=i: four(rs.at[24 + i])
-    pending["weights_x_sent"] = lambda: wait_bytes(wall, ss.at[2], 1)
-
-    def pass_on(rounds):
-        for r in rounds:
+            gather(d, i, mate, 3, 36 + r)
+
+    for r in ROUNDS:
+        for p in (1, 3, 2):
+            pending[f"weights_x{r}{p}"] = lambda n=24 + 3 * r + p - 1: wait_bytes(wall.at[0], rs.at[n], 8)
+        pending[f"weights_core{r}"] = lambda r=r: wait_bytes(wall.at[0], rs.at[36 + r], GX)
+    pending["weights_x_sent"] = lambda: wait_bytes(wall, ss.at[2], 3)
+    pending["weights_core_sent"] = lambda: wait_bytes(wall, ss.at[3], 4)
+    for r in ROUNDS:
+        for p in (1, 3, 2):
+            settle(f"weights_x{r}{p}")
             for i in (2 * r, 2 * r + 1):
-                settle(f"weights_x{i}")
-                gather(other, i, mate, 3, 3)
-
-    pass_on(ROUNDS[:2])
+                gather(lax.rem(d + 8 - 2 * p, DP), i, mate, 3, 36 + r)
 
     def to_modes(recv, scale):
         r = recv[...].reshape(512, 128)
@@ -297,12 +291,9 @@
     mall[d] = modes
     m_v[...] = modes.astype(F32)
 
-    pass_on(ROUNDS[2:])
-    expect("weights_core", 3, wall, 2)
-    settle("weights_core")
 
     def weight(a, h, oh, k):
-        return wall[2 * h + oh, k, a].astype(F32)
+        return wall[4 * a + 2 * h + oh, k].astype(F32)
 
     def mix(k, c):
         mr = [m_v[pl.ds(h * 32 + k, 1), :] for h in range(2)]
@@ -320,7 +311,11 @@
             p_v[1, pl.ds(row, 16), :] = im.astype(BF16)
         return c
 
-    lax.fori_loop(0, MX, mix, 0, unroll=8)
+    for r in ROUNDS:
+        settle(f"weights_core{r}")
+        for i in (2 * r, 2 * r + 1):
+            first = 4 * block_z(i)
+            lax.fori_loop(0, 4, lambda j, c: mix(first + j, c), 0, unroll=True)
     mixed = []
     for a in range(2):
         q = jnp.where(diag, dot(p_v[a], ones_b), 0.0).astype(BF16)
@@ -445,22 +440,27 @@
     load("gin", o_v, gin_hbm, 8)
 
     settle("wg")
-    for kyh in range(2):
-        swapped = swap16(rwg[kyh * 16:kyh * 16 + 16].astype(F32))
-        for o in range(16):
-            wo_v[:, o, kyh * 128:(kyh + 1) * 128] = swapped[o]
-    load("wg_out", wo_v, wg_hbm, 9)
+    load("wg_out", rwg, wg_hbm, 9)
     settle(*list(pending))
 
 
-def writer(out_a, gin_a, wg_a, out_b, gin_b, wg_b, sem):
+def writer(out_a, gin_a, wg_a, out_b, gin_b, wg_b, pieces, wo_v, sem):
+    first = pltpu.make_async_copy(wg_a, pieces, sem.at[9])
+    first.start()
     pairs = [(a.at[i], b.at[i]) for a, b in ((out_a, out_b), (gin_a, gin_b)) for i in range(SLAB)]
-    pairs.append((wg_a, wg_b))
     copies = [pltpu.make_async_copy(a, b, sem.at[n]) for n, (a, b) in enumerate(pairs)]
     for copy in copies:
         copy.start()
+    first.wait()
+    for kyh in range(2):
+        swapped = swap16(pieces[kyh * 16:kyh * 16 + 16].astype(F32))
+        for o in range(16):
+            wo_v[:, o, kyh * 128:(kyh + 1) * 128] = swapped[o]
+    last = pltpu.make_async_copy(wo_v, wg_b, sem.at[8])
+    last.start()
     for copy in copies:
         copy.wait()
+    last.wait()
 
 
 def per_device(inputs, spectral_weights, skip_weights, cotangent, *tabs):
@@ -478,23 +478,21 @@
     ]
     results = pl.pallas_call(
         kernel,
-        out_shape=[vm(s.shape, s.dtype) for s in shapes],
+        out_shape=[vm(shape5, BF16), vm(shape5, BF16), piece],
         in_specs=[hbm] * 9,
         out_specs=[any_spec] * 3,
         scratch_shapes=[
             big, big, big, big,
             vm((256, 1024), BF16), vm((1024, 256), BF16), vm((1024, 512), BF16),
             vm((128, 512), BF16), vm((512, 128), BF16),
-            vm((2, 16, 16, 256), BF16),
-            vm((GX, 2, 16, 128), BF16), *([piece] * 10),
-            vm((4, GX, 2, 16, 128), BF16), vm((DP, 128, 128), BF16), vm((DP, 128, 128), BF16),
+            vm((16, 16, 256), BF16),
+            *([piece] * 11),
+            vm((DP, *PIECE), BF16), vm((DP, 128, 128), BF16), vm((DP, 128, 128), BF16),
             vm((128, 128), F32), vm((2, 1024, 128), BF16), vm((2, 1024, 128), F32),
             vm((512, 256), BF16), vm((2, 256, 512), F32), vm(shape5, F32), vm((256, 1024), BF16), vm((32, 32), BF16),
-            vm(PIECE, F32), vm((16, 16, 256), F32),
+            vm(PIECE, F32),
             vm((256, 256), BF16), vm((256, 256), BF16),
-            pltpu.SemaphoreType.DMA((36,)),
-            pltpu.SemaphoreType.DMA((36,)),
-            pltpu.SemaphoreType.DMA((36,)),
+            *([pltpu.SemaphoreType.DMA((40,))] * 3),
         ],
         compiler_params=pltpu.CompilerParams(
             collective_id=0, has_side_effects=True, vmem_limit_bytes=40 * 1024 * 1024
@@ -510,8 +508,8 @@
         out_shape=shapes,
         in_specs=[any_spec] * 3,
         out_specs=[hbm] * 3,
-        scratch_shapes=[pltpu.SemaphoreType.DMA((9,))],
-        compiler_params=pltpu.CompilerParams(vmem_limit_bytes=1024 * 1024),
+        scratch_shapes=[piece, vm((16, 16, 256), F32), pltpu.SemaphoreType.DMA((10,))],
+        compiler_params=pltpu.CompilerParams(vmem_limit_bytes=4 * 1024 * 1024),
         name="write_results",
     )(*results)
     return (

time: 59.8 us -> 57.7 us (0.965)
  Pallas kernels: 59.1 us -> 57 us
    pallas_call x1, Pallas kernels: 56.9 us -> 54.6 us  [per_device(): pl.pallas_call(kernel, out_shape=[vm(shape5, BF16), vm(shape5, BF16), pie...]
where the time goes in v4:
time: 57.7 us; the launch traced here: 57.6 us
  Pallas kernels  57 us (99%)
  between operations  0.64 us (1%)
    pallas_call x1, Pallas kernels, per_device(): pl.pallas_call(kernel, out_shape=[vm(shape5, BF16), vm(shape5, BF16), pie...  54.6 us
    pallas_call x1, Pallas kernels, per_device(): pl.pallas_call(writer, out_shape=shapes, in_specs=[any_spec] * 3, out_spe...  2.34 us

profile of v4, /device:TPU:1, one launch (start us, length us, event | category | flops | bytes accessed | tf_op | source)
XLA Modules:
  0.0 57.6 jit_solution(13238498500269890571)
XLA Ops:
  0.6 54.6 %spectral_layer.1 = (bf16[4,64,2,16,128]{4,3,2,1,0:T(8,128)(2,1)S(1)}, bf16[4,64,2,16,128]{4,3,2,1,0:T(8,128)(2,1)S(1)}, bf16[32,16,128]{2,1,0:T(8,128)(2,1)S(1)}) custom-call(bf16[4,64,2,16,128]{4,3,2,1,0:T(8,128)(2,1)} %bitcast.6, bf16[2,32,32,256]{3,2,1,0:T(8,128)(2,1)} %bitcast.10, bf16[32,32]{1,0:T(8,128)(2,1)} %s_hbm.1, ...), custom_call_target="tpu_custom_call" | custom-call | flops 8000000000 | bytes 12000000 | tf_op jit(solution)/shard_map/spectral_layer/pallas_call | solution.py:479
  55.3 2.3 %write_results.1 = (bf16[4,64,2,16,128]{4,3,2,1,0:T(8,128)(2,1)}, bf16[4,64,2,16,128]{4,3,2,1,0:T(8,128)(2,1)}, f32[16,16,256]{2,1,0:T(8,128)}) custom-call(bf16[4,64,2,16,128]{4,3,2,1,0:T(8,128)(2,1)S(1)} %get-tuple-element.9.out_a, bf16[4,64,2,16,128]{4,3,2,1,0:T(8,128)(2,1)S(1)} %get-tuple-element.10.gin_a, bf16[32,16,128]{2,1,0:T(8,128)(2,1)S(1)} %get-tuple-element.11.wg_a), custom_call_target="tpu_custom_call" | custom-call | tf_op jit(solution)/shard_map/write_results/pallas_call | solution.py:506

commit v5 on v4

--- a/solution.py
+++ b/solution.py
@@ -20,7 +20,7 @@
 GRID_SCALE = 1.0 / math.sqrt(NX * NY * NZ)
 MODE_SCALE = 1.0 / math.sqrt(MX * MY * MZ)
 PIECE = (GX, 16, 128)
-ROUNDS = (3, 2, 1, 0)
+ROUNDS = (0, 1, 2, 3)
 
 
 def angles(length, freqs):
@@ -216,14 +216,14 @@
     def body_w(q, c):
         t = peer(q)
         pltpu.make_async_remote_copy(
-            sw.at[t], wall.at[d, me], ss.at[0], rs.at[20 + q // 8],
+            sw.at[t], wall.at[d, q], ss.at[0], rs.at[20 + q // 8],
             device_id={"gx": t}, device_id_type=MESH,
         ).start()
         return c
 
     for r in ROUNDS:
         lax.fori_loop(8 * r, min(8 * r + 8, GX - 1), body_w, 0, unroll=True)
-    wall[d, me] = sw[me]
+    wall[d, GX - 1] = sw[me]
     pending["weights_sent"] = lambda: wait_bytes(sw, ss.at[0], GX - 1)
     for r in ROUNDS:
         pending[f"weights_gx{r}"] = lambda r=r: wait_bytes(sw, rs.at[20 + r], min(8, GX - 1 - 8 * r))
@@ -248,24 +248,24 @@
 
     mate = d + 1 - 2 * lax.rem(d, 2)
 
-    def block_z(i):
-        return lax.rem(me // 4 + 4 - (1 - 2 * (i % 2)) * ((i + 1) // 2), 8)
-
-    def gather(s, i, target, send_n, recv_n):
-        z = block_z(i)
-        block = wall.at[s, pl.ds(4 * z, 4)]
+    def gather(s, r, target, send_n, recv_n):
+        block = wall.at[s, pl.ds(8 * r, 8)]
         pltpu.make_async_remote_copy(
             block, block, ss.at[send_n], rs.at[recv_n],
             device_id={"dp": target}, device_id_type=MESH,
         ).start()
 
+    def source(q):
+        i, j = q // 4, lax.rem(q, 4)
+        dz = 4 + (1 - 2 * lax.rem(i, 2)) * ((i + 1) // 2)
+        dy = 2 + (1 - 2 * lax.rem(j, 2)) * ((j + 1) // 2)
+        return lax.rem(me // 4 + 8 - dz, 8) * 4 + lax.rem(lax.rem(me, 4) + 4 - dy, 4)
+
     for r in ROUNDS:
         settle(f"weights_gx{r}")
         for p in (2, 1, 3):
-            for i in (2 * r, 2 * r + 1):
-                gather(d, i, lax.rem(d + 2 * p, DP), 2, 24 + 3 * r + p - 1)
-        for i in (2 * r, 2 * r + 1):
-            gather(d, i, mate, 3, 36 + r)
+            gather(d, r, lax.rem(d + 2 * p, DP), 2, 24 + 3 * r + p - 1)
+        gather(d, r, mate, 3, 36 + r)
 
     for r in ROUNDS:
         for p in (1, 3, 2):
@@ -276,8 +276,7 @@
     for r in ROUNDS:
         for p in (1, 3, 2):
             settle(f"weights_x{r}{p}")
-            for i in (2 * r, 2 * r + 1):
-                gather(lax.rem(d + 8 - 2 * p, DP), i, mate, 3, 36 + r)
+            gather(lax.rem(d + 8 - 2 * p, DP), r, mate, 3, 36 + r)
 
     def to_modes(recv, scale):
         r = recv[...].reshape(512, 128)
@@ -292,16 +291,17 @@
     m_v[...] = modes.astype(F32)
 
 
-    def weight(a, h, oh, k):
-        return wall[4 * a + 2 * h + oh, k].astype(F32)
-
-    def mix(k, c):
+    def weight(a, h, oh, q):
+        return wall[4 * a + 2 * h + oh, q].astype(F32)
+
+    def mix(q, c):
+        k = source(q)
         mr = [m_v[pl.ds(h * 32 + k, 1), :] for h in range(2)]
         mi = [m_v[pl.ds(64 + h * 32 + k, 1), :] for h in range(2)]
         for oh in range(2):
             re = im = None
             for h in range(2):
-                wr, wi = weight(0, h, oh, k), weight(1, h, oh, k)
+                wr, wi = weight(0, h, oh, q), weight(1, h, oh, q)
                 r = wr * mr[h] - wi * mi[h]
                 i = wr * mi[h] + wi * mr[h]
                 re = r if re is None else re + r
@@ -313,9 +313,7 @@
 
     for r in ROUNDS:
         settle(f"weights_core{r}")
-        for i in (2 * r, 2 * r + 1):
-            first = 4 * block_z(i)
-            lax.fori_loop(0, 4, lambda j, c: mix(first + j, c), 0, unroll=True)
+        lax.fori_loop(8 * r, 8 * r + 8, mix, 0, unroll=True)
     mixed = []
     for a in range(2):
         q = jnp.where(diag, dot(p_v[a], ones_b), 0.0).astype(BF16)
@@ -331,17 +329,14 @@
         gx_v[256:512, :] = turned.T.astype(BF16)
 
     def skips(source, channel_map):
-        def body(t, c):
-            for x in range(0, SLAB, 2):
-                src = jnp.concatenate(
-                    [source[x + i, pl.ds(t * 8, 8)].reshape(256, 128) for i in range(2)], axis=1
-                )
-                skip = dot(channel_map[...], src).reshape(8, 2, 16, 256)
-                for i in range(2):
-                    sk_v[x + i, pl.ds(t * 8, 8)] = skip[..., i * 128:(i + 1) * 128]
-            return c
-
-        lax.fori_loop(0, 8, body, 0)
+        for t in range(8):
+            rows = slice(t * 8, t * 8 + 8)
+            src = jnp.concatenate(
+                [source[x, rows].reshape(256, 128) for x in range(SLAB)], axis=1
+            )
+            skip = dot(channel_map[...], src).reshape(8, 2, 16, 512)
+            for x in range(SLAB):
+                sk_v[x, rows] = skip[..., x * 128:(x + 1) * 128]
 
     def fields(scale, emit):
         for t in range(4):
@@ -380,13 +375,14 @@
         rows = jnp.where(diag, dot(rep_l, back[64 * a:64 * a + 64]), 0.0).astype(BF16)
         q_v[a] = dot(rows, ones_b)
 
-    def conj_mix(k, c):
+    def conj_mix(q, c):
+        k = source(q)
         for h in range(2):
             re = im = None
             for oh in range(2):
                 row = pl.multiple_of(oh * 512 + k * 16, 16)
                 br, bi = q_v[0, pl.ds(row, 16), :], q_v[1, pl.ds(row, 16), :]
-                wr, wi = weight(0, h, oh, k), weight(1, h, oh, k)
+                wr, wi = weight(0, h, oh, q), weight(1, h, oh, q)
                 r = wr * br + wi * bi
                 i = wr * bi - wi * br
                 re = r if re is None else re + r
@@ -396,7 +392,7 @@
             p_v[1, pl.ds(row, 16), :] = im.astype(BF16)
         return c
 
-    lax.fori_loop(0, MX, conj_mix, 0, unroll=8)
+    lax.fori_loop(0, MX, conj_mix, 0, unroll=16)
     back_modes = [dot(sum_l, p_v[a]) for a in range(2)]
     to_slabs(jnp.concatenate(back_modes, axis=0).astype(BF16), sd2)
     spread("d2", sd2, rd2, 8)

time: 57.7 us -> 59.2 us (1.026)
  Pallas kernels: 57 us -> 58.5 us
    pallas_call x1, Pallas kernels: 54.6 us -> 56.1 us  [per_device(): pl.pallas_call(kernel, out_shape=[vm(shape5, BF16), vm(shape5, BF16), pie...]
where the time goes in v5:
time: 59.2 us; the launch traced here: 59.1 us
  Pallas kernels  58.5 us (99%)
  between operations  0.64 us (1%)
    pallas_call x1, Pallas kernels, per_device(): pl.pallas_call(kernel, out_shape=[vm(shape5, BF16), vm(shape5, BF16), pie...  56.1 us
    pallas_call x1, Pallas kernels, per_device(): pl.pallas_call(writer, out_shape=shapes, in_specs=[any_spec] * 3, out_spe...  2.34 us

profile of v5, /device:TPU:1, one launch (start us, length us, event | category | flops | bytes accessed | tf_op | source)
XLA Modules:
  0.0 59.1 jit_solution(208074442112828085)
XLA Ops:
  0.6 56.1 %spectral_layer.1 = (bf16[4,64,2,16,128]{4,3,2,1,0:T(8,128)(2,1)S(1)}, bf16[4,64,2,16,128]{4,3,2,1,0:T(8,128)(2,1)S(1)}, bf16[32,16,128]{2,1,0:T(8,128)(2,1)S(1)}) custom-call(bf16[4,64,2,16,128]{4,3,2,1,0:T(8,128)(2,1)} %bitcast.6, bf16[2,32,32,256]{3,2,1,0:T(8,128)(2,1)} %bitcast.10, bf16[32,32]{1,0:T(8,128)(2,1)} %s_hbm.1, ...), custom_call_target="tpu_custom_call" | custom-call | flops 8000000000 | bytes 12000000 | tf_op jit(solution)/shard_map/spectral_layer/pallas_call | solution.py:475
  56.8 2.3 %write_results.1 = (bf16[4,64,2,16,128]{4,3,2,1,0:T(8,128)(2,1)}, bf16[4,64,2,16,128]{4,3,2,1,0:T(8,128)(2,1)}, f32[16,16,256]{2,1,0:T(8,128)}) custom-call(bf16[4,64,2,16,128]{4,3,2,1,0:T(8,128)(2,1)S(1)} %get-tuple-element.9.out_a, bf16[4,64,2,16,128]{4,3,2,1,0:T(8,128)(2,1)S(1)} %get-tuple-element.10.gin_a, bf16[32,16,128]{2,1,0:T(8,128)(2,1)S(1)} %get-tuple-element.11.wg_a), custom_call_target="tpu_custom_call" | custom-call | tf_op jit(solution)/shard_map/write_results/pallas_call | solution.py:502
